TPU v7x, 256 devices: a whole 4x4x8 slice. The times are simulated.
256 devices in a mesh: axial: 16 (over z, core), cross: 16 (over x, y).
Axes of the slice: x: 4, y: 4, z: 8, core: 2. Of those that a mesh axis runs over, the one named last changes fastest.
Arguments:
- operator_blocks: bfloat16 [16, 16, 64, 8, 64, 64], P('axial', 'cross'), may hold values from -0.00048828125 to 0.00048828125
- prolong_blocks: bfloat16 [16, 16, 64, 64, 256], P('axial', 'cross'), may hold values from -6 to 6
- operator_cols: int32 [16, 16, 64, 8], P('axial', 'cross'), may hold values from 0 to 16383, as said below
- coarse_map: int32 [16384, 4], replicated, may hold values from 0 to 15, as said below
- live_rows: int32 [16, 16], P('axial', 'cross'), may hold values from 32 to 64, as said below
Outputs:
- coarse_matrix: float32 [1024, 1024], replicated
Inputs may be any that keep to these rules, and one draw needn't show every extreme that they name: `operator_cols`: A slot of a row in segment s and partition p names a row of partition p in segment s - 1, s or s + 1; slot 0 names the row itself. `coarse_map`: the 4 coarse blocks of one row are distinct, and for a row of segment s they lie among the 5 blocks that begin at min(max(s - 1, 0), 11). `live_rows`: some partition uses all 64 rows in every draw.
All inputs are finite; a program needn't handle non-finite values.
Results may differ from a plain program's by a relative error of at most 0.003.
Values may be sent and summed in bfloat16 or wider, within the bound.
A program may use at most 192 MiB of HBM per device.

v0:
```python
import math

import jax
import jax.numpy as jnp
from jax import lax
from jax.sharding import PartitionSpec as P

B = 64
CB = 64
NCB = 16
KP = 4
NC = 1024


def with_halo(block, sides, width):
    for axis, dim in sides:
        count = lax.axis_size(axis)
        forward = [(i, i + 1) for i in range(count - 1)]
        backward = [(target, source) for source, target in forward]
        low = lax.ppermute(
            lax.slice_in_dim(block, block.shape[dim] - width, None, axis=dim), axis, forward
        )
        high = lax.ppermute(lax.slice_in_dim(block, 0, width, axis=dim), axis, backward)
        block = jnp.concatenate([low, block, high], axis=dim)
    return block


def on_device(operator_blocks, prolong_blocks, operator_cols, coarse_map, live_rows):
    block_rows = prolong_blocks.shape[2]
    sections = lax.axis_size("cross")
    segments = lax.axis_size("axial")
    segment = lax.axis_index("axial")
    section = lax.axis_index("cross")
    window = max(NCB // segments + 2, KP + 1)
    band_blocks = min(NCB, 2 * ((window + 2 * (NCB // segments + 1) + 1) // 2))
    band_cols = band_blocks * CB
    highest = lax.Precision.HIGHEST

    def lowest_of(seg):
        return jnp.clip(seg * NCB // segments - 1, 0, NCB - window)

    own_low = lowest_of(segment)
    band_start = jnp.clip(lowest_of(jnp.maximum(segment - 1, 0)), 0, NCB - band_blocks)
    local_rows = jnp.arange(block_rows, dtype=jnp.int32)
    alive = local_rows < live_rows[0, 0]
    masked = jnp.where(
        alive[None, None, :, None, None], prolong_blocks, jnp.zeros((), jnp.bfloat16)
    )
    beside_all = with_halo(masked, (("axial", 0),), 1)
    beside_all = beside_all.reshape(3 * block_rows, B, KP, CB)
    neighbour = segment - 1 + jnp.arange(3, dtype=jnp.int32)[:, None]
    global_rows = ((neighbour * sections + section) * block_rows + local_rows[None, :]).reshape(-1)
    clipped = jnp.clip(global_rows, 0, coarse_map.shape[0] - 1)
    band_labels = band_start + jnp.arange(band_blocks, dtype=jnp.int32)
    select = (coarse_map[clipped][:, :, None] == band_labels[None, None, :]).astype(jnp.bfloat16)
    expanded = jnp.einsum("rpn,rbpc->rbnc", select, beside_all, preferred_element_type=jnp.float32)
    expanded = expanded.astype(jnp.bfloat16).reshape(3 * block_rows, B, band_cols)
    own_prolong = masked[0, 0]
    own_global = (segment * sections + section) * block_rows + local_rows
    own_labels = own_low + jnp.arange(window, dtype=jnp.int32)
    own_select = (coarse_map[own_global][:, :, None] == own_labels[None, None, :]).astype(
        jnp.float32
    )
    columns = operator_cols[0, 0]
    halo_index = (
        columns // (sections * block_rows) - segment + 1
    ) * block_rows + columns % block_rows
    blocks = operator_blocks[0, 0]
    group_size = math.gcd(block_rows, 8)

    def add_group(accumulated, group_index):
        first_row = group_index * group_size
        local_blocks = lax.dynamic_slice_in_dim(blocks, first_row, group_size, 0)
        local_index = lax.dynamic_slice_in_dim(halo_index, first_row, group_size, 0)
        picked = expanded[local_index]
        product = jnp.einsum(
            "gkab,gkbm->gam", local_blocks, picked, preferred_element_type=jnp.float32
        )
        product = product.astype(jnp.bfloat16)
        own_rows = lax.dynamic_slice_in_dim(own_prolong, first_row, group_size, 0)
        weighted = jnp.einsum("gbq,gbm->gqm", own_rows, product, preferred_element_type=jnp.float32)
        own_part = lax.dynamic_slice_in_dim(own_select, first_row, group_size, 0)
        update = jnp.einsum(
            "gpw,gpcm->wcm",
            own_part,
            weighted.reshape(group_size, KP, CB, band_cols),
            precision=highest,
        )
        return (accumulated + update.reshape(window * CB, band_cols), None)

    start_value = jnp.zeros((window * CB, band_cols), jnp.float32)
    partial_band = lax.scan(
        add_group, start_value, jnp.arange(block_rows // group_size, dtype=jnp.int32)
    )[0]
    placed = lax.dynamic_update_slice(
        jnp.zeros((NC, NC), jnp.float32), partial_band, (own_low * CB, band_start * CB)
    )
    return lax.psum(placed, ("axial", "cross"))


def solution(mesh):
    return jax.shard_map(
        on_device,
        mesh=mesh,
        in_specs=(
            P("axial", "cross", None, None, None, None),
            P("axial", "cross", None, None, None),
            P("axial", "cross", None, None),
            P(),
            P("axial", "cross"),
        ),
        out_specs=P(),
        check_vma=False,
    )
```

profile of v0, /device:TPU:1, one launch (start us, length us, event | category | flops | bytes accessed | tf_op | source)
XLA Modules:
  0.0 681.4 jit_solution(13779426666413324604)
XLA Ops:
  7.2 3.2 broadcast_select_fusion
  10.4 5.3 collective-permute-start.1
  15.6 1.9 collective-permute-start
  17.8 0.8 copy.15
  18.6 5.6 copy.13
  24.2 4.0 gather_fusion.1
  28.2 4.1 gather_fusion.2
  32.5 1.5 fusion.30
  34.0 5.4 collective-permute-done.1
  39.4 1.4 collective-permute-done
  40.8 6.4 pad_maximum_fusion
  47.2 18.7 %reshape.93 = bf16[192,64,4,64]{3,2,1,0:T(4,128)(2,1)} reshape(bf16[3,1,64,64,256]{4,3,2,1,0:T(8,128)(2,1)} %pad_maximum_fusion) | data formatting | bytes 12582912 | tf_op jit(solution)/shard_map/reshape | solution.py:50
  65.9 26.1 %convert_bitcast_fusion = bf16[192,64,10,64]{3,2,1,0:T(8,128)(2,1)} fusion(bf16[192,64,4,64]{3,2,1,0:T(4,128)(2,1)} %reshape.93, s32[10]{0:T(128)S(1)} %iota_add_fusion, s32[192,4]{1,0:T(8,128)S(1)} %gather_fusion.2), kind=kOutput, calls=%fused_computation.18 | convolution fusion | flops 70786560 | bytes 22023208 | tf_op jit(solution)/shard_map/rpn,rbpc->rbnc/dot_general | solution.py:56
  92.0 57.9 %copy.17 = bf16[192,64,10,64]{0,3,2,1:T(8,128)(2,1)} copy(bf16[192,64,10,64]{3,2,1,0:T(8,128)(2,1)} %convert_bitcast_fusion) | data formatting | bytes 31457280 | tf_op jit(solution)/shard_map/convert_element_type | solution.py:57
  149.9 28.0 %copy.18 = bf16[192,64,640]{2,1,0:T(8,128)(2,1)} copy(bf16[192,64,640]{0,2,1:T(8,128)(2,1)} %bitcast.86) | data formatting | bytes 31457280
  177.9 212.8 %while.11 = (s32[]{:T(128)}, f32[320,640]{1,0:T(8,128)S(1)}, s32[8]{0:T(128)S(1)}, f32[64,4,5]{0,2,1:T(8,128)S(1)}, bf16[64,64,256]{2,1,0:T(8,128)(2,1)}, /*inde...) while((s32[]{:T(128)}, f32[320,640]{1,0:T(8,128)S(1)}, ...), condition=%wide.region_1.2_spmd.clone, body=%wide.region_0.1_spmd.clone.sunk | while | flops 582698176 | bytes 32452296 | solution.py:92
  179.3 8.9 %gather_fusion = bf16[64,64,640]{2,1,0:T(8,128)(2,1)} fusion(bf16[192,64,640]{2,1,0:T(8,128)(2,1)} %get-tuple-element.179, s32[1024]{0:T(1024)S(1)} %pad_clamp_fusion.4), kind=kCustom, calls=%fused_computation.clone.clone.1 | custom fusion | bytes 10486016 | tf_op jit(solution)/shard_map/while/body/eval_jaxpr/gather | solution.py:75
  188.2 6.9 %fusion.46 = f32[8,256,640]{2,1,0:T(8,128)} fusion(bf16[8,8,64,640]{3,2,1,0:T(8,128)(2,1)} %bitcast.84, bf16[64,8,64,64]{3,2,1,0:T(8,128)(2,1)} %get-tuple-element.177, s32[]{:T(128)S(6)} %select_n.92, bf16[64,64,256]{2,1,0:T(8,128)(2,1)} %get-tuple-element.176), kind=kOutput, calls=%fused_computation.8.clone.1 | convolution fusion | flops 503644160 | bytes 11797504 | tf_op jit(solution)/shard_map/while/body/eval_jaxpr/gbq,gbm->gqm/dot_general | solution.py:81
  195.1 9.0 %fusion.47 = f32[5,64,640]{2,0,1:T(8,128)S(1)} fusion(f32[8,4,64,640]{3,2,1,0:T(8,128)} %bitcast.85, f32[64,4,5]{0,2,1:T(8,128)S(1)} %get-tuple-element.175, s32[]{:T(128)S(6)} %select_n.92), kind=kOutput, calls=%fused_computation.6.clone.1 | convolution fusion | flops 78643200 | bytes 6067204 | tf_op jit(solution)/shard_map/while/body/eval_jaxpr/gpw,gpcm->wcm/dot_general | solution.py:83
  204.5 0.7 dynamic_slice.40
  205.9 8.9 %gather_fusion = bf16[64,64,640]{2,1,0:T(8,128)(2,1)} fusion(bf16[192,64,640]{2,1,0:T(8,128)(2,1)} %get-tuple-element.179, s32[1024]{0:T(1024)S(1)} %pad_clamp_fusion.4), kind=kCustom, calls=%fused_computation.clone.clone.1 | custom fusion | bytes 10486016 | tf_op jit(solution)/shard_map/while/body/eval_jaxpr/gather | solution.py:75
  214.8 6.9 %fusion.46 = f32[8,256,640]{2,1,0:T(8,128)} fusion(bf16[8,8,64,640]{3,2,1,0:T(8,128)(2,1)} %bitcast.84, bf16[64,8,64,64]{3,2,1,0:T(8,128)(2,1)} %get-tuple-element.177, s32[]{:T(128)S(6)} %select_n.92, bf16[64,64,256]{2,1,0:T(8,128)(2,1)} %get-tuple-element.176), kind=kOutput, calls=%fused_computation.8.clone.1 | convolution fusion | flops 503644160 | bytes 11797504 | tf_op jit(solution)/shard_map/while/body/eval_jaxpr/gbq,gbm->gqm/dot_general | solution.py:81
  221.7 9.0 %fusion.47 = f32[5,64,640]{2,0,1:T(8,128)S(1)} fusion(f32[8,4,64,640]{3,2,1,0:T(8,128)} %bitcast.85, f32[64,4,5]{0,2,1:T(8,128)S(1)} %get-tuple-element.175, s32[]{:T(128)S(6)} %select_n.92), kind=kOutput, calls=%fused_computation.6.clone.1 | convolution fusion | flops 78643200 | bytes 6067204 | tf_op jit(solution)/shard_map/while/body/eval_jaxpr/gpw,gpcm->wcm/dot_general | solution.py:83
  231.1 0.7 dynamic_slice.40
  232.5 8.9 %gather_fusion = bf16[64,64,640]{2,1,0:T(8,128)(2,1)} fusion(bf16[192,64,640]{2,1,0:T(8,128)(2,1)} %get-tuple-element.179, s32[1024]{0:T(1024)S(1)} %pad_clamp_fusion.4), kind=kCustom, calls=%fused_computation.clone.clone.1 | custom fusion | bytes 10486016 | tf_op jit(solution)/shard_map/while/body/eval_jaxpr/gather | solution.py:75
  241.4 6.9 %fusion.46 = f32[8,256,640]{2,1,0:T(8,128)} fusion(bf16[8,8,64,640]{3,2,1,0:T(8,128)(2,1)} %bitcast.84, bf16[64,8,64,64]{3,2,1,0:T(8,128)(2,1)} %get-tuple-element.177, s32[]{:T(128)S(6)} %select_n.92, bf16[64,64,256]{2,1,0:T(8,128)(2,1)} %get-tuple-element.176), kind=kOutput, calls=%fused_computation.8.clone.1 | convolution fusion | flops 503644160 | bytes 11797504 | tf_op jit(solution)/shard_map/while/body/eval_jaxpr/gbq,gbm->gqm/dot_general | solution.py:81
  248.3 9.0 %fusion.47 = f32[5,64,640]{2,0,1:T(8,128)S(1)} fusion(f32[8,4,64,640]{3,2,1,0:T(8,128)} %bitcast.85, f32[64,4,5]{0,2,1:T(8,128)S(1)} %get-tuple-element.175, s32[]{:T(128)S(6)} %select_n.92), kind=kOutput, calls=%fused_computation.6.clone.1 | convolution fusion | flops 78643200 | bytes 6067204 | tf_op jit(solution)/shard_map/while/body/eval_jaxpr/gpw,gpcm->wcm/dot_general | solution.py:83
  259.1 8.9 %gather_fusion = bf16[64,64,640]{2,1,0:T(8,128)(2,1)} fusion(bf16[192,64,640]{2,1,0:T(8,128)(2,1)} %get-tuple-element.179, s32[1024]{0:T(1024)S(1)} %pad_clamp_fusion.4), kind=kCustom, calls=%fused_computation.clone.clone.1 | custom fusion | bytes 10486016 | tf_op jit(solution)/shard_map/while/body/eval_jaxpr/gather | solution.py:75
  268.0 6.9 %fusion.46 = f32[8,256,640]{2,1,0:T(8,128)} fusion(bf16[8,8,64,640]{3,2,1,0:T(8,128)(2,1)} %bitcast.84, bf16[64,8,64,64]{3,2,1,0:T(8,128)(2,1)} %get-tuple-element.177, s32[]{:T(128)S(6)} %select_n.92, bf16[64,64,256]{2,1,0:T(8,128)(2,1)} %get-tuple-element.176), kind=kOutput, calls=%fused_computation.8.clone.1 | convolution fusion | flops 503644160 | bytes 11797504 | tf_op jit(solution)/shard_map/while/body/eval_jaxpr/gbq,gbm->gqm/dot_general | solution.py:81
  274.9 9.0 %fusion.47 = f32[5,64,640]{2,0,1:T(8,128)S(1)} fusion(f32[8,4,64,640]{3,2,1,0:T(8,128)} %bitcast.85, f32[64,4,5]{0,2,1:T(8,128)S(1)} %get-tuple-element.175, s32[]{:T(128)S(6)} %select_n.92), kind=kOutput, calls=%fused_computation.6.clone.1 | convolution fusion | flops 78643200 | bytes 6067204 | tf_op jit(solution)/shard_map/while/body/eval_jaxpr/gpw,gpcm->wcm/dot_general | solution.py:83
  284.3 0.7 dynamic_slice.40
  285.7 8.9 %gather_fusion = bf16[64,64,640]{2,1,0:T(8,128)(2,1)} fusion(bf16[192,64,640]{2,1,0:T(8,128)(2,1)} %get-tuple-element.179, s32[1024]{0:T(1024)S(1)} %pad_clamp_fusion.4), kind=kCustom, calls=%fused_computation.clone.clone.1 | custom fusion | bytes 10486016 | tf_op jit(solution)/shard_map/while/body/eval_jaxpr/gather | solution.py:75
  294.6 6.9 %fusion.46 = f32[8,256,640]{2,1,0:T(8,128)} fusion(bf16[8,8,64,640]{3,2,1,0:T(8,128)(2,1)} %bitcast.84, bf16[64,8,64,64]{3,2,1,0:T(8,128)(2,1)} %get-tuple-element.177, s32[]{:T(128)S(6)} %select_n.92, bf16[64,64,256]{2,1,0:T(8,128)(2,1)} %get-tuple-element.176), kind=kOutput, calls=%fused_computation.8.clone.1 | convolution fusion | flops 503644160 | bytes 11797504 | tf_op jit(solution)/shard_map/while/body/eval_jaxpr/gbq,gbm->gqm/dot_general | solution.py:81
  301.5 9.0 %fusion.47 = f32[5,64,640]{2,0,1:T(8,128)S(1)} fusion(f32[8,4,64,640]{3,2,1,0:T(8,128)} %bitcast.85, f32[64,4,5]{0,2,1:T(8,128)S(1)} %get-tuple-element.175, s32[]{:T(128)S(6)} %select_n.92), kind=kOutput, calls=%fused_computation.6.clone.1 | convolution fusion | flops 78643200 | bytes 6067204 | tf_op jit(solution)/shard_map/while/body/eval_jaxpr/gpw,gpcm->wcm/dot_general | solution.py:83
  312.3 8.9 %gather_fusion = bf16[64,64,640]{2,1,0:T(8,128)(2,1)} fusion(bf16[192,64,640]{2,1,0:T(8,128)(2,1)} %get-tuple-element.179, s32[1024]{0:T(1024)S(1)} %pad_clamp_fusion.4), kind=kCustom, calls=%fused_computation.clone.clone.1 | custom fusion | bytes 10486016 | tf_op jit(solution)/shard_map/while/body/eval_jaxpr/gather | solution.py:75
  321.2 6.9 %fusion.46 = f32[8,256,640]{2,1,0:T(8,128)} fusion(bf16[8,8,64,640]{3,2,1,0:T(8,128)(2,1)} %bitcast.84, bf16[64,8,64,64]{3,2,1,0:T(8,128)(2,1)} %get-tuple-element.177, s32[]{:T(128)S(6)} %select_n.92, bf16[64,64,256]{2,1,0:T(8,128)(2,1)} %get-tuple-element.176), kind=kOutput, calls=%fused_computation.8.clone.1 | convolution fusion | flops 503644160 | bytes 11797504 | tf_op jit(solution)/shard_map/while/body/eval_jaxpr/gbq,gbm->gqm/dot_general | solution.py:81
  328.1 9.0 %fusion.47 = f32[5,64,640]{2,0,1:T(8,128)S(1)} fusion(f32[8,4,64,640]{3,2,1,0:T(8,128)} %bitcast.85, f32[64,4,5]{0,2,1:T(8,128)S(1)} %get-tuple-element.175, s32[]{:T(128)S(6)} %select_n.92), kind=kOutput, calls=%fused_computation.6.clone.1 | convolution fusion | flops 78643200 | bytes 6067204 | tf_op jit(solution)/shard_map/while/body/eval_jaxpr/gpw,gpcm->wcm/dot_general | solution.py:83
  337.5 0.7 dynamic_slice.40
  338.9 8.9 %gather_fusion = bf16[64,64,640]{2,1,0:T(8,128)(2,1)} fusion(bf16[192,64,640]{2,1,0:T(8,128)(2,1)} %get-tuple-element.179, s32[1024]{0:T(1024)S(1)} %pad_clamp_fusion.4), kind=kCustom, calls=%fused_computation.clone.clone.1 | custom fusion | bytes 10486016 | tf_op jit(solution)/shard_map/while/body/eval_jaxpr/gather | solution.py:75
  347.8 6.9 %fusion.46 = f32[8,256,640]{2,1,0:T(8,128)} fusion(bf16[8,8,64,640]{3,2,1,0:T(8,128)(2,1)} %bitcast.84, bf16[64,8,64,64]{3,2,1,0:T(8,128)(2,1)} %get-tuple-element.177, s32[]{:T(128)S(6)} %select_n.92, bf16[64,64,256]{2,1,0:T(8,128)(2,1)} %get-tuple-element.176), kind=kOutput, calls=%fused_computation.8.clone.1 | convolution fusion | flops 503644160 | bytes 11797504 | tf_op jit(solution)/shard_map/while/body/eval_jaxpr/gbq,gbm->gqm/dot_general | solution.py:81
  354.7 9.0 %fusion.47 = f32[5,64,640]{2,0,1:T(8,128)S(1)} fusion(f32[8,4,64,640]{3,2,1,0:T(8,128)} %bitcast.85, f32[64,4,5]{0,2,1:T(8,128)S(1)} %get-tuple-element.175, s32[]{:T(128)S(6)} %select_n.92), kind=kOutput, calls=%fused_computation.6.clone.1 | convolution fusion | flops 78643200 | bytes 6067204 | tf_op jit(solution)/shard_map/while/body/eval_jaxpr/gpw,gpcm->wcm/dot_general | solution.py:83
  365.5 8.9 %gather_fusion = bf16[64,64,640]{2,1,0:T(8,128)(2,1)} fusion(bf16[192,64,640]{2,1,0:T(8,128)(2,1)} %get-tuple-element.179, s32[1024]{0:T(1024)S(1)} %pad_clamp_fusion.4), kind=kCustom, calls=%fused_computation.clone.clone.1 | custom fusion | bytes 10486016 | tf_op jit(solution)/shard_map/while/body/eval_jaxpr/gather | solution.py:75
  374.4 6.9 %fusion.46 = f32[8,256,640]{2,1,0:T(8,128)} fusion(bf16[8,8,64,640]{3,2,1,0:T(8,128)(2,1)} %bitcast.84, bf16[64,8,64,64]{3,2,1,0:T(8,128)(2,1)} %get-tuple-element.177, s32[]{:T(128)S(6)} %select_n.92, bf16[64,64,256]{2,1,0:T(8,128)(2,1)} %get-tuple-element.176), kind=kOutput, calls=%fused_computation.8.clone.1 | convolution fusion | flops 503644160 | bytes 11797504 | tf_op jit(solution)/shard_map/while/body/eval_jaxpr/gbq,gbm->gqm/dot_general | solution.py:81
  381.3 9.0 %fusion.47 = f32[5,64,640]{2,0,1:T(8,128)S(1)} fusion(f32[8,4,64,640]{3,2,1,0:T(8,128)} %bitcast.85, f32[64,4,5]{0,2,1:T(8,128)S(1)} %get-tuple-element.175, s32[]{:T(128)S(6)} %select_n.92), kind=kOutput, calls=%fused_computation.6.clone.1 | convolution fusion | flops 78643200 | bytes 6067204 | tf_op jit(solution)/shard_map/while/body/eval_jaxpr/gpw,gpcm->wcm/dot_general | solution.py:83
  390.7 2.5 broadcast_in_dim.18
  393.2 5.7 dynamic_update_slice.3
  398.9 270.8 %all-reduce.2.cloned.1.call-done = f32[1024,1024]{1,0:T(8,128)} async-done(((f32[1024,1024]{1,0:T(8,128)}), f32[1024,1024]{1,0:T(8,128)}) %all-reduce.2.cloned.1.call-update) | async-done | bytes 4194320 | tf_op jit(solution)/shard_map/psum | solution.py:98
  669.8 4.8 copy.39
  (63 shorter events, 6.4 us)
Async XLA Ops:
  6.5 663.2 %all-reduce.2.cloned.1.call-start = ((), (), s32[]{:S(2)}) async-start(), calls=%async_computation | async-start | bytes 8388608 | tf_op jit(solution)/shard_map/psum | solution.py:98
  10.4 22.1 %copy-start = (bf16[1,1,64,64,256]{4,3,2,1,0:T(8,128)(2,1)S(1)}, bf16[1,1,64,64,256]{4,3,2,1,0:T(8,128)(2,1)}, u32[]{:S(2)}) copy-start(bf16[1,1,64,64,256]{4,3,2,1,0:T(8,128)(2,1)} %param.8) | copy-start | bytes 6291460
  10.4 29.1 %collective-permute-start.1 = (bf16[1,1,64,64,256]{4,3,2,1,0:T(8,128)(2,1)}, bf16[1,1,64,64,256]{4,3,2,1,0:T(8,128)(2,1)}, u32[]{:S(2)}, u32[]{:S(2)}) collective-permute-start(bf16[1,1,64,64,256]{4,3,2,1,0:T(8,128)(2,1)} %broadcast_select_fusion), channel_id=1, source_target_pairs={{16,0},{32,16},{48,32},{64,48},{80,64},{96,80},{112,96},{128,112},... | collective-permute-start | bytes 6291464 | tf_op jit(solution)/shard_map/ppermute | solution.py:23
  15.6 25.2 %collective-permute-start = (bf16[1,1,64,64,256]{4,3,2,1,0:T(8,128)(2,1)}, bf16[1,1,64,64,256]{4,3,2,1,0:T(8,128)(2,1)}, u32[]{:S(2)}, u32[]{:S(2)}) collective-permute-start(bf16[1,1,64,64,256]{4,3,2,1,0:T(8,128)(2,1)} %broadcast_select_fusion), channel_id=1, source_target_pairs={{0,16},{16,32},{32,48},{48,64},{64,80},{80,96},{96,112},{112,128},... | collective-permute-start | bytes 6291464 | tf_op jit(solution)/shard_map/ppermute | solution.py:20
Sparse Core Ops, SparseCore 0:
  399.1 270.6 all-reduce.1
where the time goes:
time: 686 us; the launch traced here: 681 us
  waiting for transfers between devices  278 us (41%)
  local copies, waits for them, and re-layouts  211 us (31%)
  matrix products  154 us (22%)
  between operations  14.2 us (2%)
  other arithmetic  12.7 us (2%)
  starting transfers between devices  7.19 us (1%)
    psum x1, waiting for transfers between devices, on_device(): return lax.psum(placed, ('axial', 'cross'))  271 us
    dot_general x8, matrix products, add_group(): jnp.einsum('gpw,gpcm->wcm', own_part, weighted.reshape(group_size, KP, CB...  72.1 us
    gather x8, local copies, waits for them, and re-layouts, add_group(): picked = expanded[local_index]  71.2 us
    convert_element_type x1, local copies, waits for them, and re-layouts, on_device(): expanded.astype(jnp.bfloat16).reshape(3 * block_rows, B, band_cols)  57.9 us
    dot_general x8, matrix products, add_group(): jnp.einsum('gbq,gbm->gqm', own_rows, product, preferred_element_type=jnp....  55.4 us
    unnamed x6, local copies, waits for them, and re-layouts  39.2 us
    dot_general x1, matrix products, on_device(): jnp.einsum('rpn,rbpc->rbnc', select, beside_all, preferred_element_type=j...  26.1 us
    reshape x1, local copies, waits for them, and re-layouts, on_device(): beside_all = beside_all.reshape(3 * block_rows, B, KP, CB)  18.7 us
  transfers between devices with their start and end apart: 3, of which 3 were waited for; matrix products, arithmetic and copies ran while one was open for 2% of the time, Pallas kernels for 0%

commit v1 on v0

v1 whole, which is shorter than its diff:
```python
import functools

import jax
import jax.numpy as jnp
from jax import lax
from jax.experimental import pallas as pl
from jax.experimental.pallas import tpu as pltpu
from jax.sharding import PartitionSpec as P

NCB = 16
W = 5
ROWS = 64
MESH = pl.DeviceIdType.MESH
GROUP = 8


def lowest_of(segment):
    return jnp.clip(segment - 1, 0, NCB - W)


def base_of(segment):
    low = lowest_of(jnp.maximum(segment - 1, 0))
    return jnp.minimum(low - low % 2, 8)


def local_kernel(cols, table, own_table, base_half, a_ref, low_ref, own_ref, high_ref, out_ref, tiles, wide, left, product, total):
    step = pl.program_id(0)
    lane_low = lax.broadcasted_iota(jnp.int32, (64, 128), 1) < 64

    @pl.when(step == 0)
    def _():
        tiles[12 * ROWS] = jnp.zeros((64, 128), jnp.bfloat16)
        for part, ref in enumerate((low_ref, own_ref, high_ref)):

            @pl.loop(0, ROWS, unroll=4)
            def _(row, part=part, ref=ref):
                value = ref[row]
                at = 4 * (part * ROWS + row)
                for pair in range(2):
                    tile = value[:, 128 * pair : 128 * pair + 128]
                    tiles[at + pair] = tile
                    tiles[at + 2 + pair] = jnp.concatenate([tile[:, 64:], tile[:, :64]], axis=1)

        @pl.loop(0, 3 * ROWS, unroll=4)
        def _(row):
            for pair in range(4):
                wide[row, :, 128 * pair : 128 * pair + 128] = jnp.where(
                    lane_low, tiles[table[2 * pair, row]], tiles[table[2 * pair + 1, row]]
                )

        total[...] = jnp.zeros_like(total)

    @pl.loop(0, GROUP, unroll=2)
    def _(inner):
        row = step * GROUP + inner
        value = None
        for half in range(2):
            slots = range(4 * half, 4 * half + 4)
            lhs = jnp.concatenate([a_ref[inner, k] for k in slots], axis=1)
            rhs = jnp.concatenate([wide[cols[k, row]] for k in slots], axis=0)
            term = jnp.dot(lhs, rhs, preferred_element_type=jnp.float32)
            value = term if value is None else value + term
        at = pl.ds(pl.multiple_of(inner * 64, 64), 64)
        product[at, :] = value.astype(jnp.bfloat16)
        for pair in range(3):
            left[at, 128 * pair : 128 * pair + 128] = jnp.where(
                lane_low, tiles[own_table[2 * pair, row]], tiles[own_table[2 * pair + 1, row]]
            )

    total[...] += lax.dot_general(
        left[...], product[...], (((0,), (0,)), ((), ())), preferred_element_type=jnp.float32
    )

    @pl.when(step == pl.num_programs(0) - 1)
    def _():
        for quarter in range(4):
            for pair in range(4):
                target = quarter * 4 + lax.rem(base_half[0] + pair, 4)
                for block in range(W):
                    at = block * 64 + quarter * 16
                    out_ref[target, block * 16 : block * 16 + 16, :] = total[
                        at : at + 16, 128 * pair : 128 * pair + 128
                    ].astype(jnp.bfloat16)


def local_part(cols, table, own_table, base_half, blocks, low, own, high):
    smem = pl.BlockSpec(memory_space=pltpu.SMEM)
    whole = pl.BlockSpec((ROWS, 64, 256), lambda i: (0, 0, 0))
    return pl.pallas_call(
        local_kernel,
        grid=(ROWS // GROUP,),
        out_shape=jax.ShapeDtypeStruct((16, 80, 128), jnp.bfloat16),
        in_specs=[
            smem,
            smem,
            smem,
            smem,
            pl.BlockSpec((GROUP, 8, 64, 64), lambda i: (i, 0, 0, 0)),
            whole,
            whole,
            whole,
        ],
        out_specs=pl.BlockSpec((16, 80, 128), lambda i: (0, 0, 0)),
        scratch_shapes=[
            pltpu.VMEM((12 * ROWS + 1, 64, 128), jnp.bfloat16),
            pltpu.VMEM((3 * ROWS, 64, 512), jnp.bfloat16),
            pltpu.VMEM((GROUP * 64, 384), jnp.bfloat16),
            pltpu.VMEM((GROUP * 64, 512), jnp.bfloat16),
            pltpu.VMEM((384, 512), jnp.float32),
        ],
        compiler_params=pltpu.CompilerParams(vmem_limit_bytes=56 * 2**20),
        name="local_part",
    )(cols, table, own_table, base_half, blocks, low, own, high)


def sum_kernel(chunks, gathered, from_cross, from_axial, ready, units, sent, got, sent2, got2, sent3, got3, sent4, got4, sent5, got5):
    seg = lax.axis_index("axial")
    sec = lax.axis_index("cross")
    core = lax.rem(seg, 2)
    layer = seg // 2
    quarter = lax.rem(sec, 4)
    sibling = seg + 1 - 2 * core

    barrier = pltpu.get_barrier_semaphore()
    for d in range(1, 16):
        pl.semaphore_signal(barrier, inc=1, device_id=(seg, lax.rem(sec + d, 16)), device_id_type=MESH)
        pl.semaphore_signal(barrier, inc=1, device_id=(lax.rem(seg + d, 16), sec), device_id_type=MESH)
    pl.semaphore_wait(barrier, 30)

    def cross_copy(d):
        target = lax.rem(sec + d, 16)
        return pltpu.make_async_remote_copy(
            src_ref=chunks.at[target],
            dst_ref=from_cross.at[d],
            send_sem=sent.at[d],
            recv_sem=got.at[d],
            device_id=(seg, target),
            device_id_type=MESH,
        )

    for d in range(1, 16):
        cross_copy(d).start()
    value = chunks[sec].astype(jnp.float32)
    for d in range(1, 16):
        cross_copy(d).wait_recv()
        value = value + from_cross[d].astype(jnp.float32)
    units[0:80, :] = value
    units[80:112, :] = jnp.zeros((32, 128), jnp.float32)

    def half_of(segment):
        start = base_of(segment) // 2
        return (start + lax.rem(quarter - start + 8, 4)) // 4

    my_half = half_of(seg)
    my_low = lowest_of(seg)

    def axial_copy(i):
        block = my_low + i
        owner = (block // 2) * 2 + my_half
        return owner, lax.rem(block, 2), pltpu.make_async_remote_copy(
            src_ref=units.at[pl.ds(16 * i, 16)],
            dst_ref=from_axial.at[seg, lax.rem(block, 2)],
            send_sem=sent2.at[i],
            recv_sem=got2.at[seg, lax.rem(block, 2)],
            device_id=(owner, sec),
            device_id_type=MESH,
        )

    for i in range(W):
        owner, place, copy = axial_copy(i)

        @pl.when(owner != seg)
        def _(copy=copy):
            copy.start()

        @pl.when(owner == seg)
        def _(i=i, place=place):
            from_axial[seg, place] = units[16 * i : 16 * i + 16, :]

    @pl.loop(0, 16)
    def _(source):
        low = lowest_of(source)
        for place in range(2):
            block = 2 * layer + place

            @pl.when((half_of(source) == core) & (block >= low) & (block < low + W))
            def _(place=place):
                @pl.when(source != seg)
                def _():
                    pltpu.make_async_remote_copy(
                        src_ref=units.at[pl.ds(0, 16)],
                        dst_ref=from_axial.at[source, place],
                        send_sem=sent2.at[0],
                        recv_sem=got2.at[source, place],
                        device_id=(sibling, sec),
                        device_id_type=MESH,
                    ).wait_recv()

                units[80 + 16 * place : 96 + 16 * place, :] += from_axial[source, place]

    mine = pl.ds(pl.multiple_of(layer * 32, 32), 32)
    ready[mine, :] = units[80:112, :].astype(jnp.bfloat16)

    def layer_copy(d):
        return pltpu.make_async_remote_copy(
            src_ref=ready.at[mine],
            dst_ref=ready.at[mine],
            send_sem=sent3.at[d],
            recv_sem=got3.at[d],
            device_id=(lax.rem(seg + 2 * d, 16), sec),
            device_id_type=MESH,
        )

    for d in range(1, 8):
        layer_copy(d).start()
    for d in range(1, 8):
        source = pl.ds(pl.multiple_of(lax.rem(layer - d + 8, 8) * 32, 32), 32)
        pltpu.make_async_remote_copy(
            src_ref=ready.at[source],
            dst_ref=ready.at[source],
            send_sem=sent3.at[d],
            recv_sem=got3.at[d],
            device_id=(sibling, sec),
            device_id_type=MESH,
        ).wait_recv()

    first = jnp.where(core == 0, quarter // 3, jnp.minimum(3 + quarter, 4))
    gathered[core, sec] = ready[pl.ds(pl.multiple_of(first * 16, 16), 192), :]

    def share_copy(d):
        return pltpu.make_async_remote_copy(
            src_ref=gathered.at[core, sec],
            dst_ref=gathered.at[core, sec],
            send_sem=sent4.at[d],
            recv_sem=got4.at[d],
            device_id=(seg, lax.rem(sec + d, 16)),
            device_id_type=MESH,
        )

    def pass_copy(half, d):
        section = lax.rem(sec - d + 16, 16)
        return pltpu.make_async_remote_copy(
            src_ref=gathered.at[half, section],
            dst_ref=gathered.at[half, section],
            send_sem=sent5.at[d],
            recv_sem=got5.at[d],
            device_id=(sibling, sec),
            device_id_type=MESH,
        )

    for d in range(1, 16):
        share_copy(d).start()
    pass_copy(core, 0).start()
    for d in range(1, 16):
        section = lax.rem(sec - d + 16, 16)
        pltpu.make_async_remote_copy(
            src_ref=gathered.at[core, section],
            dst_ref=gathered.at[core, section],
            send_sem=sent4.at[d],
            recv_sem=got4.at[d],
            device_id=(sibling, sec),
            device_id_type=MESH,
        ).wait_recv()
        pass_copy(core, d).start()
    for d in range(16):
        pass_copy(1 - core, d).wait_recv()

    for d in range(1, 16):
        cross_copy(d).wait_send()
        share_copy(d).wait_send()
    for d in range(1, 8):
        layer_copy(d).wait_send()
    for d in range(16):
        pass_copy(core, d).wait_send()
    for i in range(W):
        owner, _, copy = axial_copy(i)

        @pl.when(owner != seg)
        def _(copy=copy):
            copy.wait_send()


def sum_over_devices(chunks):
    dma = pltpu.SemaphoreType.DMA
    vmem = pl.BlockSpec(memory_space=pltpu.VMEM)
    return pl.pallas_call(
        sum_kernel,
        out_shape=jax.ShapeDtypeStruct((2, 16, 192, 128), jnp.bfloat16),
        in_specs=[vmem],
        out_specs=vmem,
        scratch_shapes=[
            pltpu.VMEM((16, 80, 128), jnp.bfloat16),
            pltpu.VMEM((16, 2, 16, 128), jnp.float32),
            pltpu.VMEM((256, 128), jnp.bfloat16),
            pltpu.VMEM((112, 128), jnp.float32),
            dma((16,)),
            dma((16,)),
            dma((W,)),
            dma((16, 2)),
            dma((8,)),
            dma((8,)),
            dma((16,)),
            dma((16,)),
            dma((16,)),
            dma((16,)),
        ],
        compiler_params=pltpu.CompilerParams(
            collective_id=0, has_side_effects=True, vmem_limit_bytes=16 * 2**20
        ),
        name="sum_over_devices",
    )(chunks)


def place_kernel(shares, out_ref):
    out_ref[...] = jnp.zeros_like(out_ref)
    for half in range(2):
        for quarter in range(4):
            first = quarter // 3 if half == 0 else min(3 + quarter, 4)
            for part in range(4):
                for unit in range(12):
                    row = (first + unit) * 64 + part * 16
                    column = (quarter + 4 * half) * 128
                    out_ref[row : row + 16, column : column + 128] = shares[
                        half, part * 4 + quarter, unit * 16 : unit * 16 + 16, :
                    ].astype(jnp.float32)


def place(shares):
    vmem = pl.BlockSpec(memory_space=pltpu.VMEM)
    return pl.pallas_call(
        place_kernel,
        out_shape=jax.ShapeDtypeStruct((1024, 1024), jnp.float32),
        in_specs=[vmem],
        out_specs=vmem,
        compiler_params=pltpu.CompilerParams(vmem_limit_bytes=16 * 2**20),
        name="place",
    )(shares)


def tables(operator_cols, coarse_map, live, segment, section):
    base = base_of(segment)
    order = jnp.arange(3 * ROWS, dtype=jnp.int32)
    labels = []
    for offset in (-1, 0, 1):
        near = jnp.clip(segment + offset, 0, 15)
        labels.append(lax.dynamic_slice(coarse_map.T, (0, (near * 16 + section) * ROWS), (4, ROWS)))
    labels = jnp.concatenate(labels, axis=1)
    alive = (order % ROWS) < jnp.repeat(live, ROWS)
    source = jnp.array([[0, 2, 1, 3], [2, 0, 3, 1]], jnp.int32)

    def find(labels, wanted, alive, order):
        hit = labels[None, :, :] == wanted[:, None, None]
        tile = jnp.tile(source, (wanted.shape[0] // 2, 1))[:, :, None]
        found = jnp.sum(jnp.where(hit, 4 * order[None, None, :] + tile, 0), axis=1)
        return jnp.where(jnp.any(hit, axis=1) & alive[None, :], found, 12 * ROWS)

    table = find(labels, base + jnp.arange(8, dtype=jnp.int32), alive, order)
    own = slice(ROWS, 2 * ROWS)
    own_table = find(
        labels[:, own],
        jnp.concatenate([lowest_of(segment) + jnp.arange(W, dtype=jnp.int32), jnp.full((1,), -1, jnp.int32)]),
        alive[own],
        order[own],
    )
    columns = operator_cols[0, 0].T
    columns = (columns // (16 * ROWS) - segment + 1) * ROWS + columns % ROWS
    return columns, table, own_table, jnp.reshape(base // 2, (1,))


def on_device(operator_blocks, prolong_blocks, operator_cols, coarse_map, live_rows):
    segment = lax.axis_index("axial")
    section = lax.axis_index("cross")
    forward = [(i, i + 1) for i in range(15)]
    backward = [(i + 1, i) for i in range(15)]
    own = prolong_blocks[0, 0]
    low = lax.ppermute(own, "axial", forward)
    high = lax.ppermute(own, "axial", backward)
    live = live_rows[0]
    live = jnp.concatenate([lax.ppermute(live, "axial", forward), live, lax.ppermute(live, "axial", backward)])
    columns, table, own_table, base_half = tables(operator_cols, coarse_map, live, segment, section)
    chunks = local_part(columns, table, own_table, base_half, operator_blocks[0, 0], low, own, high)
    return place(sum_over_devices(chunks))


def solution(mesh):
    return jax.shard_map(
        on_device,
        mesh=mesh,
        in_specs=(
            P("axial", "cross", None, None, None, None),
            P("axial", "cross", None, None, None),
            P("axial", "cross", None, None),
            P(),
            P("axial", "cross"),
        ),
        out_specs=P(),
        check_vma=False,
    )
```

time: 686 us -> 107 us (0.16)
  waiting for transfers between devices: 278 us -> 15.7 us
  local copies, waits for them, and re-layouts: 211 us -> 3.48 us
  matrix products: 154 us -> 0 us
  Pallas kernels: 0 us -> 70.2 us
  between operations: 14.2 us -> 0.78 us
  other arithmetic: 12.7 us -> 4.38 us
    psum x1 -> x0, waiting for transfers between devices: 271 us -> none  [on_device(): return lax.psum(placed, ('axial', 'cross'))]
    dot_general x17 -> x0, matrix products: 154 us -> none  [the longest x8 72.1 us: add_group(): jnp.einsum('gpw,gpcm->wcm', own_part, weighted.reshape(group_size, KP, CB...]
    gather x11 -> x0, local copies, waits for them, and re-layouts: 79.3 us -> none  [the longest x8 71.2 us: add_group(): picked = expanded[local_index]]
    pallas_call x0 -> x3, Pallas kernels: none -> 70.2 us  [the longest x1 39.7 us: sum_over_devices(): pl.pallas_call(sum_kernel, out_shape=jax.ShapeDtypeStruct((2, 16, 192, 12...]
    convert_element_type x1 -> x0, local copies, waits for them, and re-layouts: 57.9 us -> none  [on_device(): expanded.astype(jnp.bfloat16).reshape(3 * block_rows, B, band_cols)]
    unnamed x6 -> x4, local copies, waits for them, and re-layouts: 39.2 us -> 1 us
    reshape x1, local copies, waits for them, and re-layouts: 18.7 us -> 0.08 us  [tables(): alive = order % ROWS < jnp.repeat(live, ROWS)]
    ppermute x2 -> x4, waiting for transfers between devices: 6.8 us -> 15.7 us  [the longest x1 14.4 us: on_device(): high = lax.ppermute(own, 'axial', backward)]
  transfers between devices with their start and end apart: 3 -> 4, of which waited for: 3 -> 2; matrix products, arithmetic and copies ran while one was open for 2% -> 6% of each run, Pallas kernels for 0% -> 0%
where the time goes in v1:
time: 107 us
  Pallas kernels  70.2 us (66%)
  waiting for transfers between devices  15.7 us (15%)
  starting transfers between devices  12.6 us (12%)
  other arithmetic  4.38 us (4%)
  local copies, waits for them, and re-layouts  3.48 us (3%)
    pallas_call x1, Pallas kernels, sum_over_devices(): pl.pallas_call(sum_kernel, out_shape=jax.ShapeDtypeStruct((2, 16, 192, 12...  39.7 us
    pallas_call x1, Pallas kernels, local_part(): pl.pallas_call(local_kernel, grid=(ROWS // GROUP,), out_shape=jax.ShapeDt...  28 us
    ppermute x1, waiting for transfers between devices, on_device(): high = lax.ppermute(own, 'axial', backward)  14.4 us
    ppermute x1, starting transfers between devices, on_device(): lax.ppermute(live, 'axial', backward)  5.14 us
    ppermute x1, starting transfers between devices, on_device(): high = lax.ppermute(own, 'axial', backward)  2.9 us
    ppermute x1, starting transfers between devices, on_device(): low = lax.ppermute(own, 'axial', forward)  2.67 us
    pallas_call x1, Pallas kernels, place(): pl.pallas_call(place_kernel, out_shape=jax.ShapeDtypeStruct((1024, 1024),...  2.49 us
  transfers between devices with their start and end apart: 4, of which 2 were waited for; matrix products, arithmetic and copies ran while one was open for 6% of the time, Pallas kernels for 0%

profile of v1, /device:TPU:1, one launch (start us, length us, event | category | flops | bytes accessed | tf_op | source)
XLA Modules:
  0.0 107.1 jit_solution(31137793589544917)
XLA Ops:
  0.0 5.1 %collective-permute-start.1 = (s32[1]{0:T(128)}, s32[1]{0:T(128)}, u32[]{:S(2)}, u32[]{:S(2)}) collective-permute-start(s32[1]{0:T(128)} %bitcast.6), channel_id=1, source_target_pairs={{16,0},{32,16},{48,32},{64,48},{80,64},{96,80},{112,96},{128,112},... | collective-permute-start | bytes 20 | tf_op jit(solution)/shard_map/ppermute | solution.py:379
  5.1 1.9 %collective-permute-start = (s32[1]{0:T(128)}, s32[1]{0:T(128)}, u32[]{:S(2)}, u32[]{:S(2)}) collective-permute-start(s32[1]{0:T(128)} %bitcast.6), channel_id=1, source_target_pairs={{0,16},{16,32},{32,48},{48,64},{64,80},{80,96},{96,112},{112,128},... | collective-permute-start | bytes 20 | tf_op jit(solution)/shard_map/ppermute | solution.py:379
  7.1 2.9 %collective-permute-start.3 = (bf16[64,64,256]{2,1,0:T(8,128)(2,1)}, bf16[64,64,256]{2,1,0:T(8,128)(2,1)S(1)}, u32[]{:S(2)}, u32[]{:S(2)}) collective-permute-start(bf16[64,64,256]{2,1,0:T(8,128)(2,1)} %bitcast.41), channel_id=1, source_target_pairs={{16,0},{32,16},{48,32},{64,48},{80,64},{96,80},{112,96},{128,112},... | collective-permute-start | bytes 6291464 | tf_op jit(solution)/shard_map/ppermute | solution.py:377
  10.0 2.7 %collective-permute-start.2 = (bf16[64,64,256]{2,1,0:T(8,128)(2,1)}, bf16[64,64,256]{2,1,0:T(8,128)(2,1)}, u32[]{:S(2)}, u32[]{:S(2)}) collective-permute-start(bf16[64,64,256]{2,1,0:T(8,128)(2,1)} %bitcast.42), channel_id=1, source_target_pairs={{0,16},{16,32},{32,48},{48,64},{64,80},{80,96},{96,112},{112,128},... | collective-permute-start | bytes 6291464 | tf_op jit(solution)/shard_map/ppermute | solution.py:376
  13.4 0.7 tile.18
  14.1 0.7 tile.16
  14.8 0.1 copy.7
  14.8 0.1 pad_add_fusion.2
  14.9 0.8 dynamic-slice_bitcast_fusion.2
  15.7 0.1 pad_add_fusion
  15.8 0.1 compare_reduce_fusion.1
  15.9 0.1 compare_reduce_fusion
  16.0 0.1 slice_multiply_fusion
  16.0 0.1 fusion.1
  16.1 0.1 fusion
  16.2 1.3 %fusion.6.cols = s32[8,64]{1,0:T(8,128)} fusion(s32[1,1,64,8]{2,3,1,0:T(8,128)} %param.8, s32[]{:T(128)S(6)} %axis_index.23), kind=kLoop, calls=%fused_computation.17 | loop fusion | flops 13824 | bytes 4100 | tf_op jit(solution)/shard_map/add | solution.py:366
  17.5 0.0 collective-permute-done.1
  17.5 0.0 collective-permute-done
  17.5 1.3 %pad_add_fusion.1 = s32[3]{0:T(128)S(1)} fusion(s32[1]{0:T(128)} %collective-permute-done.1, s32[1]{0:T(128)} %bitcast.39, s32[1]{0:T(128)} %collective-permute-done), kind=kLoop, calls=%fused_computation.31 | loop fusion | flops 6 | bytes 24 | tf_op jit(solution)/shard_map/concatenate | solution.py:379
  18.8 0.1 broadcast_in_dim.27
  18.9 0.1 reshape.46
  19.0 0.1 slice.6
  19.1 0.6 and_select_fusion.1.own_table
  19.7 0.6 and_select_fusion.table
  20.3 14.4 %collective-permute-done.3.high_ref = bf16[64,64,256]{2,1,0:T(8,128)(2,1)S(1)} collective-permute-done((bf16[64,64,256]{2,1,0:T(8,128)(2,1)}, bf16[64,64,256]{2,1,0:T(8,128)(2,1)S(1)}, u32[]{:S(2)}, u32[]{:S(2)}) %collective-permute-start.3) | collective-permute-done | bytes 2097184 | tf_op jit(solution)/shard_map/ppermute | solution.py:377
  34.6 0.0 copy-start.1
  34.6 1.3 %collective-permute-done.2.low_ref = bf16[64,64,256]{2,1,0:T(8,128)(2,1)} collective-permute-done((bf16[64,64,256]{2,1,0:T(8,128)(2,1)}, bf16[64,64,256]{2,1,0:T(8,128)(2,1)}, u32[]{:S(2)}, u32[]{:S(2)}) %collective-permute-start.2) | collective-permute-done | bytes 2097184 | tf_op jit(solution)/shard_map/ppermute | solution.py:376
  35.9 0.0 copy-done.1
  36.0 28.0 %local_part.1.chunks = bf16[16,80,128]{2,1,0:T(8,128)(2,1)} custom-call(s32[8,64]{1,0:T(8,128)} %fusion.6.cols, s32[8,192]{1,0:T(8,128)} %and_select_fusion.table, s32[6,64]{1,0:T(8,128)} %and_select_fusion.1.own_table, s32[1]{0:T(128)} %bitcast.8.base_half, bf16[64,8,64,64]{3,2,1,0:T(8,128)(2,1)} %bitcast.40, ...), custom_call_target="tpu_custom_call" | custom-call | tf_op jit(solution)/shard_map/local_part/pallas_call | solution.py:89
  64.0 0.0 copy-start
  64.0 1.0 copy-done
  65.0 39.7 %sum_over_devices.1.shares = bf16[2,16,192,128]{3,2,1,0:T(8,128)(2,1)S(1)} custom-call(bf16[16,80,128]{2,1,0:T(8,128)(2,1)S(1)} %copy-done), custom_call_target="tpu_custom_call" | custom-call | tf_op jit(solution)/shard_map/sum_over_devices/pallas_call | solution.py:286
  104.7 2.5 %place.1 = f32[1024,1024]{1,0:T(8,128)} custom-call(bf16[2,16,192,128]{3,2,1,0:T(8,128)(2,1)S(1)} %sum_over_devices.1.shares), custom_call_target="tpu_custom_call" | custom-call | tf_op jit(solution)/shard_map/place/pallas_call | solution.py:330
  (6 shorter events, 0.0 us)
Async XLA Ops:
  0.0 17.5 %collective-permute-start.1 = (s32[1]{0:T(128)}, s32[1]{0:T(128)}, u32[]{:S(2)}, u32[]{:S(2)}) collective-permute-start(s32[1]{0:T(128)} %bitcast.6), channel_id=1, source_target_pairs={{16,0},{32,16},{48,32},{64,48},{80,64},{96,80},{112,96},{128,112},... | collective-permute-start | bytes 20 | tf_op jit(solution)/shard_map/ppermute | solution.py:379
  5.1 12.4 %collective-permute-start = (s32[1]{0:T(128)}, s32[1]{0:T(128)}, u32[]{:S(2)}, u32[]{:S(2)}) collective-permute-start(s32[1]{0:T(128)} %bitcast.6), channel_id=1, source_target_pairs={{0,16},{16,32},{32,48},{48,64},{64,80},{80,96},{96,112},{112,128},... | collective-permute-start | bytes 20 | tf_op jit(solution)/shard_map/ppermute | solution.py:379
  7.1 27.6 %collective-permute-start.3 = (bf16[64,64,256]{2,1,0:T(8,128)(2,1)}, bf16[64,64,256]{2,1,0:T(8,128)(2,1)S(1)}, u32[]{:S(2)}, u32[]{:S(2)}) collective-permute-start(bf16[64,64,256]{2,1,0:T(8,128)(2,1)} %bitcast.41), channel_id=1, source_target_pairs={{16,0},{32,16},{48,32},{64,48},{80,64},{96,80},{112,96},{128,112},... | collective-permute-start | bytes 6291464 | tf_op jit(solution)/shard_map/ppermute | solution.py:377
  10.0 25.9 %collective-permute-start.2 = (bf16[64,64,256]{2,1,0:T(8,128)(2,1)}, bf16[64,64,256]{2,1,0:T(8,128)(2,1)}, u32[]{:S(2)}, u32[]{:S(2)}) collective-permute-start(bf16[64,64,256]{2,1,0:T(8,128)(2,1)} %bitcast.42), channel_id=1, source_target_pairs={{0,16},{16,32},{32,48},{48,64},{64,80},{80,96},{96,112},{112,128},... | collective-permute-start | bytes 6291464 | tf_op jit(solution)/shard_map/ppermute | solution.py:376
  34.6 1.3 %copy-start.1 = (bf16[64,64,256]{2,1,0:T(8,128)(2,1)}, bf16[64,64,256]{2,1,0:T(8,128)(2,1)S(1)}, u32[]{:S(2)}) copy-start(bf16[64,64,256]{2,1,0:T(8,128)(2,1)S(1)} %collective-permute-done.3.high_ref) | copy-start | bytes 6291460
  64.0 1.0 copy-start

commit v2 on v0

v2 whole, which is shorter than its diff:
```python
import jax
import jax.numpy as jnp
from jax import lax
from jax.experimental import pallas as pl
from jax.experimental.pallas import tpu as pltpu
from jax.sharding import PartitionSpec as P

NCB = 16
W = 5
ROWS = 64
CHUNKS = 4
MESH = pl.DeviceIdType.MESH
EMPTY = 4 * ROWS


def lowest_of(segment):
    return jnp.clip(segment - 1, 0, NCB - W)


def base_of(segment):
    low = lowest_of(jnp.maximum(segment - 1, 0))
    return jnp.minimum(low - low % 2, 8)


def fused_kernel(
    live, cols_ref, map_ref, p_ref, a_ref, gathered,
    maps, tab, own, near, far, blocks, beside, tiles, wide, left, product, total,
    chunks, from_cross, from_axial, ready, units,
    tab_s, load, sent0, got0, sent1, got1, sent2, got2, sent3, got3, sent4, got4, sent5, got5, sent6, got6,
):
    seg = lax.axis_index("axial")
    sec = lax.axis_index("cross")
    core = lax.rem(seg, 2)
    layer = seg // 2
    x = sec // 4
    y = lax.rem(sec, 4)
    sibling = seg + 1 - 2 * core
    beyond = seg - 1 + 2 * core
    has_far = (beyond >= 0) & (beyond < 16)
    beyond = jnp.clip(beyond, 0, 15)
    lane_off = lax.rem(sec, 2) * 64

    def remote(src, dst, send, recv, to):
        return pltpu.make_async_remote_copy(
            src_ref=src, dst_ref=dst, send_sem=send, recv_sem=recv, device_id=to, device_id_type=MESH
        )

    barrier = pltpu.get_barrier_semaphore()
    for d in range(1, 16):
        pl.semaphore_signal(barrier, inc=1, device_id=(lax.rem(seg + d, 16), sec), device_id_type=MESH)
        pl.semaphore_signal(barrier, inc=1, device_id=(seg, lax.rem(sec + d, 16)), device_id_type=MESH)

    step = ROWS // CHUNKS
    own_loads = []
    for c in range(CHUNKS):
        rows = pl.ds(step * c, step)
        own_loads.append(pltpu.make_async_copy(p_ref.at[rows], own.at[rows], load.at[c]))
        own_loads[c].start()
    map_loads = []
    for part, near_seg in enumerate((seg, sibling, beyond)):
        start = pl.multiple_of((near_seg * 16 + sec - lax.rem(sec, 2)) * ROWS, 128)
        map_loads.append(pltpu.make_async_copy(map_ref.at[:, pl.ds(start, 128)], maps.at[part], load.at[CHUNKS + part]))
        map_loads[part].start()
    block_loads = []
    for c in range(2):
        rows = pl.ds(32 * c, 32)
        block_loads.append(pltpu.make_async_copy(a_ref.at[rows], blocks.at[rows], load.at[CHUNKS + 3 + c]))
        block_loads[c].start()

    def near_copy(c):
        rows = pl.ds(step * c, step)
        return remote(own.at[rows], near.at[rows], sent0.at[0, c], got0.at[0, c], (sibling, sec))

    def far_copy(c):
        rows = pl.ds(step * c, step)
        return remote(own.at[rows], far.at[rows], sent0.at[1, c], got0.at[1, c], (beyond, sec))

    in_use = live[0, 0]
    for c in range(CHUNKS):
        own_loads[c].wait()

        @pl.loop(step * c, step * c + step, unroll=4)
        def _(row):
            own[row] = jnp.where(row < in_use, own[row], jnp.zeros((64, 256), jnp.bfloat16))

        if c == 0:
            pl.semaphore_wait(barrier, 30)

        @pl.when(has_far)
        def _(c=c):
            far_copy(c).start()

    for c in range(CHUNKS):
        near_copy(c).start()

    slot = lax.broadcasted_iota(jnp.int32, (8, 128), 0)
    local = lax.broadcasted_iota(jnp.int32, (8, 128), 1) - lane_off
    odd = lax.rem(slot, 2)

    def find(labels, first):
        found = jnp.full((8, 128), EMPTY, jnp.int32)
        for b in range(4):
            even_tile, odd_tile = (0, 2, 1, 3)[b], (2, 0, 3, 1)[b]
            tile = even_tile + odd * (odd_tile - even_tile)
            found = jnp.where(labels[b : b + 1, :] - first == slot, 4 * local + tile, found)
        return found

    base = base_of(seg)
    for part in range(3):
        map_loads[part].wait()
        labels = maps[part]
        tab[part] = find(labels, base)
        if part == 0:
            tab[3] = find(labels, lowest_of(seg))
    named = cols_ref[...]
    named_seg = lax.shift_right_logical(named, 10)
    part = jnp.where(named_seg == seg, 0, jnp.where(named_seg == sibling, 1, 2))
    tab[4, :, 0:64] = part * ROWS + (named & 63)
    tab[4, :, 64:128] = jnp.zeros((8, 64), jnp.int32)
    to_smem = pltpu.make_async_copy(tab, tab_s, load.at[CHUNKS + 5])
    to_smem.start()

    lane_low = lax.broadcasted_iota(jnp.int32, (64, 128), 1) < 64
    tiles[EMPTY] = jnp.zeros((64, 128), jnp.bfloat16)

    def half_tiles(which, row, pair):
        return jnp.where(
            lane_low,
            tiles[tab_s[which, 2 * pair, lane_off + row]],
            tiles[tab_s[which, 2 * pair + 1, lane_off + row]],
        )

    def store_tiles(source, first, count):
        @pl.loop(first, first + count, unroll=4)
        def _(row):
            value = source[row]
            for pair in range(2):
                tile = value[:, 128 * pair : 128 * pair + 128]
                tiles[4 * row + pair] = tile
                tiles[4 * row + 2 + pair] = jnp.concatenate([tile[:, 64:], tile[:, :64]], axis=1)

    def widen(part, first, count):
        @pl.loop(first, first + count, unroll=4)
        def _(row):
            for pair in range(4):
                wide[part * ROWS + row, :, 128 * pair : 128 * pair + 128] = half_tiles(part, row, pair)

    store_tiles(own, 0, ROWS)
    to_smem.wait()
    widen(0, 0, ROWS)

    @pl.loop(0, ROWS, unroll=4)
    def _(row):
        for pair in range(3):
            left[pl.ds(pl.multiple_of(row * 64, 64), 64), 128 * pair : 128 * pair + 128] = half_tiles(3, row, pair)

    for c in range(2):
        block_loads[c].wait()

        @pl.loop(32 * c, 32 * c + 32, unroll=2)
        def _(row):
            for pair in range(4):
                beside[row, :, 128 * pair : 128 * pair + 128] = jnp.concatenate(
                    [blocks[row, 2 * pair], blocks[row, 2 * pair + 1]], axis=1
                )

    for c in range(CHUNKS):
        near_copy(c).wait_recv()
    store_tiles(near, 0, ROWS)
    widen(1, 0, ROWS)

    for c in range(CHUNKS):

        @pl.when(has_far)
        def _(c=c):
            far_copy(c).wait_recv()
            store_tiles(far, step * c, step)
            widen(2, step * c, step)

    @pl.loop(0, ROWS, unroll=2)
    def _(row):
        value = None
        for half in range(2):
            rhs = jnp.concatenate([wide[tab_s[4, k, row]] for k in range(4 * half, 4 * half + 4)], axis=0)
            term = jnp.dot(
                beside[row, :, 256 * half : 256 * half + 256], rhs, preferred_element_type=jnp.float32
            )
            value = term if value is None else value + term
        product[pl.ds(pl.multiple_of(row * 64, 64), 64), :] = value.astype(jnp.bfloat16)

    def cross_send(target):
        return remote(chunks.at[target], from_cross.at[sec], sent1.at[target], got1.at[sec], (seg, target))

    for half in range(2):
        columns = slice(256 * half, 256 * half + 256)
        total[...] = jnp.zeros_like(total)

        @pl.loop(0, 8)
        def _(group, columns=columns):
            rows = pl.ds(pl.multiple_of(group * 512, 512), 512)
            total[...] += lax.dot_general(
                left[rows, :], product[rows, columns], (((0,), (0,)), ((), ())), preferred_element_type=jnp.float32
            )

        for quarter in range(4):
            for pair in range(2):
                target = quarter * 4 + lax.rem(base // 2 + 2 * half + pair, 4)
                for block in range(W):
                    at = block * 64 + quarter * 16
                    chunks[target, block * 16 : block * 16 + 16, :] = total[
                        at : at + 16, 128 * pair : 128 * pair + 128
                    ].astype(jnp.bfloat16)

                @pl.when(target != sec)
                def _(target=target):
                    cross_send(target).start()

    value = chunks[sec].astype(jnp.float32)
    for d in range(1, 16):
        source = lax.rem(sec + d, 16)
        remote(chunks.at[source], from_cross.at[source], sent1.at[source], got1.at[source], (seg, source)).wait_recv()
        value = value + from_cross[source].astype(jnp.float32)
    units[0:80, :] = value
    units[80:112, :] = jnp.zeros((32, 128), jnp.float32)

    def half_of(segment):
        start = base_of(segment) // 2
        return (start + lax.rem(y - start + 8, 4)) // 4

    my_half = half_of(seg)
    my_low = lowest_of(seg)

    def axial_copy(i):
        block = my_low + i
        owner = (block // 2) * 2 + my_half
        place = lax.rem(block, 2)
        copy = remote(
            units.at[pl.ds(16 * i, 16)], from_axial.at[seg, place], sent2.at[i], got2.at[seg, place], (owner, sec)
        )
        return owner, place, copy

    for i in range(W):
        owner, place, copy = axial_copy(i)

        @pl.when(owner != seg)
        def _(copy=copy):
            copy.start()

        @pl.when(owner == seg)
        def _(i=i, place=place):
            from_axial[seg, place] = units[16 * i : 16 * i + 16, :]

    @pl.loop(0, 16)
    def _(source):
        low = lowest_of(source)
        for place in range(2):
            block = 2 * layer + place

            @pl.when((half_of(source) == core) & (block >= low) & (block < low + W))
            def _(place=place):
                @pl.when(source != seg)
                def _():
                    remote(
                        units.at[pl.ds(0, 16)],
                        from_axial.at[source, place],
                        sent2.at[0],
                        got2.at[source, place],
                        (sibling, sec),
                    ).wait_recv()

                units[80 + 16 * place : 96 + 16 * place, :] += from_axial[source, place]

    mine = pl.ds(pl.multiple_of(layer * 32, 32), 32)
    ready[mine, :] = units[80:112, :].astype(jnp.bfloat16)

    def layer_copy(d):
        return remote(ready.at[mine], ready.at[mine], sent3.at[d], got3.at[d], (lax.rem(seg + 2 * d, 16), sec))

    for d in range(1, 8):
        layer_copy(d).start()
    for d in range(1, 8):
        source = pl.ds(pl.multiple_of(lax.rem(layer - d + 8, 8) * 32, 32), 32)
        remote(ready.at[source], ready.at[source], sent3.at[d], got3.at[d], (sibling, sec)).wait_recv()

    first = jnp.where(core == 0, y // 3, jnp.minimum(3 + y, 4))
    gathered[core, 0, y, x] = ready[pl.ds(pl.multiple_of(first * 16, 16), 96), :]
    gathered[core, 1, x, y] = ready[pl.ds(pl.multiple_of(first * 16 + 96, 16), 96), :]

    def moved(which, d):
        return (seg, lax.rem(x + d, 4) * 4 + y) if which == 0 else (seg, x * 4 + lax.rem(y + d, 4))

    def back(which, d):
        return lax.rem((x if which == 0 else y) - d + 4, 4)

    def one_copy(which, d):
        major, minor = (y, x) if which == 0 else (x, y)
        share = gathered.at[core, which, major, minor]
        return remote(share, share, sent4.at[which, d], got4.at[which, d], moved(which, d))

    def four_copy(which, d):
        shares = gathered.at[core, which, y if which == 0 else x]
        return remote(shares, shares, sent5.at[which, d], got5.at[which, d], moved(1 - which, d))

    def pass_copy(half, which, d):
        shares = gathered.at[half, which, back(1 - which, d)]
        return remote(shares, shares, sent6.at[which, d], got6.at[which, d], (sibling, sec))

    for d in (2, 1, 3):
        for which in range(2):
            one_copy(which, d).start()
    for which in range(2):
        for d in (1, 3, 2):
            share = gathered.at[core, which, y if which == 0 else x, back(which, d)]
            remote(share, share, sent4.at[which, d], got4.at[which, d], (sibling, sec)).wait_recv()
        for d in (2, 1, 3):
            four_copy(which, d).start()
    for which in range(2):
        pass_copy(core, which, 0).start()
    for d in (1, 3, 2):
        for which in range(2):
            shares = gathered.at[core, which, back(1 - which, d)]
            remote(shares, shares, sent5.at[which, d], got5.at[which, d], (sibling, sec)).wait_recv()
            pass_copy(core, which, d).start()
    for which in range(2):
        for d in range(4):
            pass_copy(1 - core, which, d).wait_recv()

    for c in range(CHUNKS):
        near_copy(c).wait_send()

        @pl.when(has_far)
        def _(c=c):
            far_copy(c).wait_send()

    for d in range(1, 16):
        cross_send(lax.rem(sec + d, 16)).wait_send()
    for i in range(W):
        owner, _, copy = axial_copy(i)

        @pl.when(owner != seg)
        def _(copy=copy):
            copy.wait_send()

    for d in range(1, 8):
        layer_copy(d).wait_send()
    for which in range(2):
        for d in range(1, 4):
            one_copy(which, d).wait_send()
            four_copy(which, d).wait_send()
        for d in range(4):
            pass_copy(core, which, d).wait_send()


def fused(live, cols, coarse, prolong, operator):
    dma = pltpu.SemaphoreType.DMA
    vmem = pl.BlockSpec(memory_space=pltpu.VMEM)
    anywhere = pl.BlockSpec(memory_space=pl.ANY)
    bf16, f32, i32 = jnp.bfloat16, jnp.float32, jnp.int32
    return pl.pallas_call(
        fused_kernel,
        out_shape=jax.ShapeDtypeStruct((2, 2, 4, 4, 96, 128), bf16),
        in_specs=[pl.BlockSpec(memory_space=pltpu.SMEM), vmem, anywhere, anywhere, anywhere],
        out_specs=vmem,
        scratch_shapes=[
            pltpu.VMEM((3, 4, 128), i32),
            pltpu.VMEM((5, 8, 128), i32),
            pltpu.VMEM((ROWS, 64, 256), bf16),
            pltpu.VMEM((ROWS, 64, 256), bf16),
            pltpu.VMEM((ROWS, 64, 256), bf16),
            pltpu.VMEM((ROWS, 8, 64, 64), bf16),
            pltpu.VMEM((ROWS, 64, 512), bf16),
            pltpu.VMEM((4 * ROWS + 1, 64, 128), bf16),
            pltpu.VMEM((3 * ROWS, 64, 512), bf16),
            pltpu.VMEM((ROWS * 64, 384), bf16),
            pltpu.VMEM((ROWS * 64, 512), bf16),
            pltpu.VMEM((384, 256), f32),
            pltpu.VMEM((16, 80, 128), bf16),
            pltpu.VMEM((16, 80, 128), bf16),
            pltpu.VMEM((16, 2, 16, 128), f32),
            pltpu.VMEM((256, 128), bf16),
            pltpu.VMEM((112, 128), f32),
            pltpu.SMEM((5, 8, 128), i32),
            dma((CHUNKS + 6,)),
            dma((2, CHUNKS)),
            dma((2, CHUNKS)),
            dma((16,)),
            dma((16,)),
            dma((W,)),
            dma((16, 2)),
            dma((8,)),
            dma((8,)),
            dma((2, 4)),
            dma((2, 4)),
            dma((2, 4)),
            dma((2, 4)),
            dma((2, 4)),
            dma((2, 4)),
        ],
        compiler_params=pltpu.CompilerParams(collective_id=0, has_side_effects=True, vmem_limit_bytes=58 * 2**20),
        name="fused",
    )(live, cols, coarse, prolong, operator)


def place_kernel(shares, out_ref):
    out_ref[...] = jnp.zeros_like(out_ref)
    for half in range(2):
        for y in range(4):
            first = y // 3 if half == 0 else min(3 + y, 4)
            for x in range(4):
                for unit in range(12):
                    row = (first + unit) * 64 + x * 16
                    column = (y + 4 * half) * 128
                    at = (half, 0, y, x) if unit < 6 else (half, 1, x, y)
                    out_ref[row : row + 16, column : column + 128] = shares[
                        (*at, slice(unit % 6 * 16, unit % 6 * 16 + 16), slice(None))
                    ].astype(jnp.float32)


def place(shares):
    vmem = pl.BlockSpec(memory_space=pltpu.VMEM)
    return pl.pallas_call(
        place_kernel,
        out_shape=jax.ShapeDtypeStruct((1024, 1024), jnp.float32),
        in_specs=[vmem],
        out_specs=vmem,
        compiler_params=pltpu.CompilerParams(vmem_limit_bytes=16 * 2**20),
        name="place",
    )(shares)


def on_device(operator_blocks, prolong_blocks, operator_cols, coarse_map, live_rows):
    shares = fused(live_rows, operator_cols[0, 0].T, coarse_map.T, prolong_blocks[0, 0], operator_blocks[0, 0])
    return place(shares)


def solution(mesh):
    return jax.shard_map(
        on_device,
        mesh=mesh,
        in_specs=(
            P("axial", "cross", None, None, None, None),
            P("axial", "cross", None, None, None),
            P("axial", "cross", None, None),
            P(),
            P("axial", "cross"),
        ),
        out_specs=P(),
        check_vma=False,
    )
```

time: 686 us -> 84.4 us (0.12)
  waiting for transfers between devices: 278 us -> 0 us
  local copies, waits for them, and re-layouts: 211 us -> 1.4 us
  matrix products: 154 us -> 0 us
  Pallas kernels: 0 us -> 82.2 us
  between operations: 14.2 us -> 0.67 us
  other arithmetic: 12.7 us -> 0 us
  starting transfers between devices: 7.19 us -> 0 us
    psum x1 -> x0, waiting for transfers between devices: 271 us -> none  [on_device(): return lax.psum(placed, ('axial', 'cross'))]
    dot_general x17 -> x0, matrix products: 154 us -> none  [the longest x8 72.1 us: add_group(): jnp.einsum('gpw,gpcm->wcm', own_part, weighted.reshape(group_size, KP, CB...]
    pallas_call x0 -> x2, Pallas kernels: none -> 82.2 us  [the longest x1 79.7 us: fused(): pl.pallas_call(fused_kernel, out_shape=jax.ShapeDtypeStruct((2, 2, 4, 4,...]
    gather x11 -> x0, local copies, waits for them, and re-layouts: 79.3 us -> none  [the longest x8 71.2 us: add_group(): picked = expanded[local_index]]
    convert_element_type x1 -> x0, local copies, waits for them, and re-layouts: 57.9 us -> none  [on_device(): expanded.astype(jnp.bfloat16).reshape(3 * block_rows, B, band_cols)]
    unnamed x6 -> x2, local copies, waits for them, and re-layouts: 39.2 us -> 1.4 us
    reshape x1 -> x0, local copies, waits for them, and re-layouts: 18.7 us -> none  [on_device(): beside_all = beside_all.reshape(3 * block_rows, B, KP, CB)]
    ppermute x2 -> x0, starting transfers between devices: 7.19 us -> none  [the longest x1 5.27 us: with_halo(): lax.ppermute(lax.slice_in_dim(block, 0, width, axis=dim), axis, backward)]
  transfers between devices with their start and end apart: 3 -> 0, of which waited for: 3 -> 0; matrix products, arithmetic and copies ran while one was open for 2% -> 0% of each run, Pallas kernels for 0% -> 0%
where the time goes in v2:
time: 84.4 us; the launch traced here: 84.3 us
  Pallas kernels  82.2 us (97%)
  local copies, waits for them, and re-layouts  1.4 us (2%)
    pallas_call x1, Pallas kernels, fused(): pl.pallas_call(fused_kernel, out_shape=jax.ShapeDtypeStruct((2, 2, 4, 4,...  79.7 us
    pallas_call x1, Pallas kernels, place(): pl.pallas_call(place_kernel, out_shape=jax.ShapeDtypeStruct((1024, 1024),...  2.49 us

profile of v2, /device:TPU:1, one launch (start us, length us, event | category | flops | bytes accessed | tf_op | source)
XLA Modules:
  0.0 84.3 jit_solution(16249563172627781981)
XLA Ops:
  0.7 79.7 %fused.1.shares = bf16[2,2,4,4,96,128]{5,4,3,2,1,0:T(8,128)(2,1)} custom-call(s32[1,1]{1,0:T(1,128)S(6)} %copy.6.live, s32[8,64]{1,0:T(8,128)} %bitcast.9, s32[4,16384]{1,0:T(4,128)} %bitcast.8, bf16[64,64,256]{2,1,0:T(8,128)(2,1)} %bitcast.7, bf16[64,8,64,64]{3,2,1,0:T(8,128)(2,1)} %bitcast.6), custom_call_target="tpu_custom_call" | custom-call | tf_op jit(solution)/shard_map/fused/pallas_call | solution.py:359
  80.4 0.0 copy-start
  80.4 1.4 %copy-done = bf16[2,2,4,4,96,128]{5,4,3,2,1,0:T(8,128)(2,1)S(1)} copy-done((bf16[2,2,4,4,96,128]{5,4,3,2,1,0:T(8,128)(2,1)S(1)}, bf16[2,2,4,4,96,128]{5,4,3,2,1,0:T(8,128)(2,1)}, u32[]{:S(2)}) %copy-start) | copy-done | bytes 1572888
  81.8 2.5 %place.1 = f32[1024,1024]{1,0:T(8,128)} custom-call(bf16[2,2,4,4,96,128]{5,4,3,2,1,0:T(8,128)(2,1)S(1)} %copy-done), custom_call_target="tpu_custom_call" | custom-call | tf_op jit(solution)/shard_map/place/pallas_call | solution.py:421
Async XLA Ops:
  80.4 1.4 %copy-start = (bf16[2,2,4,4,96,128]{5,4,3,2,1,0:T(8,128)(2,1)S(1)}, bf16[2,2,4,4,96,128]{5,4,3,2,1,0:T(8,128)(2,1)}, u32[]{:S(2)}) copy-start(bf16[2,2,4,4,96,128]{5,4,3,2,1,0:T(8,128)(2,1)} %fused.1.shares) | copy-start | bytes 4718596

commit v3 on v2

v3 whole, which is shorter than its diff:
```python
import jax
import jax.numpy as jnp
from jax import lax
from jax.experimental import pallas as pl
from jax.experimental.pallas import tpu as pltpu
from jax.sharding import PartitionSpec as P

NCB = 16
W = 5
ROWS = 64
PIECES = ((0, 32), (32, 48), (48, 64))
CHUNKS = len(PIECES)
MESH = pl.DeviceIdType.MESH
EMPTY = 4 * ROWS


def lowest_of(segment):
    return jnp.clip(segment - 1, 0, NCB - W)


def base_of(segment):
    low = lowest_of(jnp.maximum(segment - 1, 0))
    return jnp.minimum(low - low % 2, 8)


def fused_kernel(
    live, cols_ref, map_ref, p_ref, a_ref, shares_out,
    maps, tab, own, near, far, blocks, beside, tiles, wide, left, turned, partial, product, total, gathered,
    chunks, from_cross, from_axial, ready, units,
    tab_s, load, sent0, got0, sent1, got1, sent2, got2, sent3, got3, sent4, got4, sent5, got5, sent6, got6, flush,
):
    seg = lax.axis_index("axial")
    sec = lax.axis_index("cross")
    core = lax.rem(seg, 2)
    layer = seg // 2
    x = sec // 4
    y = lax.rem(sec, 4)
    sibling = seg + 1 - 2 * core
    beyond = seg - 1 + 2 * core
    has_far = (beyond >= 0) & (beyond < 16)
    beyond = jnp.clip(beyond, 0, 15)
    lane_off = lax.rem(sec, 2) * 64

    def remote(src, dst, send, recv, to):
        return pltpu.make_async_remote_copy(
            src_ref=src, dst_ref=dst, send_sem=send, recv_sem=recv, device_id=to, device_id_type=MESH
        )

    barrier = pltpu.get_barrier_semaphore()
    for d in range(1, 16):
        pl.semaphore_signal(barrier, inc=1, device_id=(lax.rem(seg + d, 16), sec), device_id_type=MESH)
        pl.semaphore_signal(barrier, inc=1, device_id=(seg, lax.rem(sec + d, 16)), device_id_type=MESH)

    def piece(ref, c):
        return ref.at[:, pl.ds(PIECES[c][0], PIECES[c][1] - PIECES[c][0]), :]

    own_loads = [pltpu.make_async_copy(piece(p_ref, c), piece(own, c), load.at[c]) for c in range(CHUNKS)]
    for copy in own_loads:
        copy.start()
    map_loads = []
    for part, near_seg in enumerate((seg, sibling, beyond)):
        start = pl.multiple_of((near_seg * 16 + sec - lax.rem(sec, 2)) * ROWS, 128)
        map_loads.append(pltpu.make_async_copy(map_ref.at[:, pl.ds(start, 128)], maps.at[part], load.at[CHUNKS + part]))
        map_loads[part].start()

    def block_load(c):
        return pltpu.make_async_copy(a_ref.at[pl.ds(16 * c, 16)], blocks.at[c % 2], load.at[CHUNKS + 3 + c])

    for c in range(2):
        block_load(c).start()

    def near_copy():
        return remote(own, near, sent0.at[CHUNKS], got0.at[CHUNKS], (sibling, sec))

    def far_copy(c):
        return remote(piece(own, c), piece(far, c), sent0.at[c], got0.at[c], (beyond, sec))

    in_use = live[0, 0]
    for c, (lo, hi) in enumerate(PIECES):
        own_loads[c].wait()

        @pl.loop(0, ROWS, unroll=8)
        def _(row, lo=lo, hi=hi):
            own[row, lo:hi, :] = jnp.where(row < in_use, own[row, lo:hi, :], jnp.zeros((hi - lo, 256), jnp.bfloat16))

        if c == 0:
            pl.semaphore_wait(barrier, 30)

        @pl.when(has_far)
        def _(c=c):
            far_copy(c).start()

    near_copy().start()

    slot = lax.broadcasted_iota(jnp.int32, (8, 128), 0)
    local = lax.broadcasted_iota(jnp.int32, (8, 128), 1) - lane_off
    odd = lax.rem(slot, 2)

    def find(labels, first):
        found = jnp.full((8, 128), EMPTY, jnp.int32)
        for b in range(4):
            even_tile, odd_tile = (0, 2, 1, 3)[b], (2, 0, 3, 1)[b]
            tile = even_tile + odd * (odd_tile - even_tile)
            found = jnp.where(labels[b : b + 1, :] - first == slot, 4 * local + tile, found)
        return found

    base = base_of(seg)
    for part in range(3):
        map_loads[part].wait()
        labels = maps[part]
        tab[part] = find(labels, base)
        if part == 0:
            tab[3] = find(labels, lowest_of(seg))
    named = cols_ref[...]
    named_seg = lax.shift_right_logical(named, 10)
    part = jnp.where(named_seg == seg, 0, jnp.where(named_seg == sibling, 1, 2))
    tab[4, :, 0:64] = part * ROWS + (named & 63)
    tab[4, :, 64:128] = jnp.zeros((8, 64), jnp.int32)
    to_smem = pltpu.make_async_copy(tab, tab_s, load.at[CHUNKS + 7])
    to_smem.start()

    lane_low = lax.broadcasted_iota(jnp.int32, (64, 128), 1) < 64
    tiles[EMPTY] = jnp.zeros((64, 128), jnp.bfloat16)

    def half_tiles(which, row, pair, lo, hi):
        return jnp.where(
            lane_low[lo:hi, :],
            tiles[tab_s[which, 2 * pair, lane_off + row], lo:hi, :],
            tiles[tab_s[which, 2 * pair + 1, lane_off + row], lo:hi, :],
        )

    def store_tiles(source, lo, hi):
        @pl.loop(0, ROWS, unroll=4)
        def _(row):
            value = source[row, lo:hi, :]
            for pair in range(2):
                tile = value[:, 128 * pair : 128 * pair + 128]
                tiles[4 * row + pair, lo:hi, :] = tile
                tiles[4 * row + 2 + pair, lo:hi, :] = jnp.concatenate([tile[:, 64:], tile[:, :64]], axis=1)

    def widen(part, lo, hi):
        @pl.loop(0, ROWS, unroll=4)
        def _(row):
            for pair in range(4):
                wide[part * ROWS + row, lo:hi, 128 * pair : 128 * pair + 128] = half_tiles(part, row, pair, lo, hi)

    store_tiles(own, 0, 64)
    to_smem.wait()
    widen(0, 0, 64)

    @pl.loop(0, 8)
    def _(group):
        for inner in range(8):
            for pair in range(3):
                left[64 * inner : 64 * inner + 64, 128 * pair : 128 * pair + 128] = half_tiles(
                    3, group * 8 + inner, pair, 0, 64
                )
        turned[group] = left[...].T

    for c in range(4):
        block_load(c).wait()

        @pl.loop(0, 16, unroll=2)
        def _(row, c=c):
            at = 0
            for lo, hi in PIECES:
                width = 8 * (hi - lo)
                beside[16 * c + row, :, at : at + width] = jnp.concatenate(
                    [blocks[c % 2, row, k][:, lo:hi] for k in range(8)], axis=1
                )
                at += width

        if c < 2:
            block_load(c + 2).start()

    near_copy().wait_recv()
    store_tiles(near, 0, 64)
    widen(1, 0, 64)

    for c, (lo, hi) in enumerate(PIECES):

        @pl.when(has_far)
        def _(c=c, lo=lo, hi=hi):
            far_copy(c).wait_recv()
            store_tiles(far, lo, hi)
            widen(2, lo, hi)

        @pl.loop(0, ROWS, unroll=4)
        def _(row, c=c, lo=lo, hi=hi):
            rhs = jnp.concatenate([wide[tab_s[4, k, row], lo:hi, :] for k in range(8)], axis=0)
            term = jnp.dot(beside[row, :, 8 * lo : 8 * hi], rhs, preferred_element_type=jnp.float32)
            at = pl.ds(pl.multiple_of(row * 64, 64), 64)
            if c > 0:
                term = partial[at, :] + term
            if c < CHUNKS - 1:
                partial[at, :] = term
            else:
                product[at, :] = term.astype(jnp.bfloat16)

    def cross_send(target):
        return remote(chunks.at[target], from_cross.at[sec], sent1.at[target], got1.at[sec], (seg, target))

    for half in range(2):
        columns = slice(256 * half, 256 * half + 256)
        value = None
        for group in range(8):
            term = jnp.dot(
                turned[group], product[512 * group : 512 * group + 512, columns], preferred_element_type=jnp.float32
            )
            value = term if value is None else value + term
        total[...] = value

        for quarter in range(4):
            for pair in range(2):
                target = quarter * 4 + lax.rem(base // 2 + 2 * half + pair, 4)
                for block in range(W):
                    at = block * 64 + quarter * 16
                    chunks[target, block * 16 : block * 16 + 16, :] = total[
                        at : at + 16, 128 * pair : 128 * pair + 128
                    ].astype(jnp.bfloat16)

                @pl.when(target != sec)
                def _(target=target):
                    cross_send(target).start()

    value = chunks[sec].astype(jnp.float32)
    for d in range(1, 16):
        source = lax.rem(sec + d, 16)
        remote(chunks.at[source], from_cross.at[source], sent1.at[source], got1.at[source], (seg, source)).wait_recv()
        value = value + from_cross[source].astype(jnp.float32)
    units[0:80, :] = value
    units[80:112, :] = jnp.zeros((32, 128), jnp.float32)

    def half_of(segment):
        start = base_of(segment) // 2
        return (start + lax.rem(y - start + 8, 4)) // 4

    my_half = half_of(seg)
    my_low = lowest_of(seg)

    def axial_copy(i):
        block = my_low + i
        owner = (block // 2) * 2 + my_half
        place = lax.rem(block, 2)
        copy = remote(
            units.at[pl.ds(16 * i, 16)], from_axial.at[seg, place], sent2.at[i], got2.at[seg, place], (owner, sec)
        )
        return owner, place, copy

    for i in range(W):
        owner, place, copy = axial_copy(i)

        @pl.when(owner != seg)
        def _(copy=copy):
            copy.start()

        @pl.when(owner == seg)
        def _(i=i, place=place):
            from_axial[seg, place] = units[16 * i : 16 * i + 16, :]

    @pl.loop(0, 16)
    def _(source):
        low = lowest_of(source)
        for place in range(2):
            block = 2 * layer + place

            @pl.when((half_of(source) == core) & (block >= low) & (block < low + W))
            def _(place=place):
                @pl.when(source != seg)
                def _():
                    remote(
                        units.at[pl.ds(0, 16)],
                        from_axial.at[source, place],
                        sent2.at[0],
                        got2.at[source, place],
                        (sibling, sec),
                    ).wait_recv()

                units[80 + 16 * place : 96 + 16 * place, :] += from_axial[source, place]

    mine = pl.ds(pl.multiple_of(layer * 32, 32), 32)
    ready[mine, :] = units[80:112, :].astype(jnp.bfloat16)

    def layer_copy(d):
        return remote(ready.at[mine], ready.at[mine], sent3.at[d], got3.at[d], (lax.rem(seg + 2 * d, 16), sec))

    for d in range(1, 8):
        layer_copy(d).start()
    for d in range(1, 8):
        source = pl.ds(pl.multiple_of(lax.rem(layer - d + 8, 8) * 32, 32), 32)
        remote(ready.at[source], ready.at[source], sent3.at[d], got3.at[d], (sibling, sec)).wait_recv()

    first = jnp.where(core == 0, y // 3, jnp.minimum(3 + y, 4))
    gathered[0, y, x] = ready[pl.ds(pl.multiple_of(first * 16, 16), 96), :]
    gathered[1, x, y] = ready[pl.ds(pl.multiple_of(first * 16 + 96, 16), 96), :]

    def moved(which, d):
        return (seg, lax.rem(x + d, 4) * 4 + y) if which == 0 else (seg, x * 4 + lax.rem(y + d, 4))

    def back(which, d):
        return lax.rem((x if which == 0 else y) - d + 4, 4)

    def one_copy(which, d):
        major, minor = (y, x) if which == 0 else (x, y)
        share = gathered.at[which, major, minor]
        return remote(share, share, sent4.at[which, d], got4.at[which, d], moved(which, d))

    def four_copy(which, d):
        shares = gathered.at[which, y if which == 0 else x]
        return remote(shares, shares, sent5.at[which, d], got5.at[which, d], moved(1 - which, d))

    def pass_copy(half, which, d):
        place = back(1 - which, d)
        shares = gathered.at[which, place]
        return remote(shares, shares_out.at[half, which, place], sent6.at[which, d], got6.at[which, d], (sibling, sec))

    def keep_copy(which, d):
        place = back(1 - which, d)
        return pltpu.make_async_copy(gathered.at[which, place], shares_out.at[core, which, place], flush.at[which, d])

    for d in (2, 1, 3):
        for which in range(2):
            one_copy(which, d).start()
    for which in range(2):
        for d in (1, 3, 2):
            share = gathered.at[which, y if which == 0 else x, back(which, d)]
            remote(share, share, sent4.at[which, d], got4.at[which, d], (sibling, sec)).wait_recv()
        for d in (2, 1, 3):
            four_copy(which, d).start()
    for which in range(2):
        pass_copy(core, which, 0).start()
        keep_copy(which, 0).start()
    for d in (1, 3, 2):
        for which in range(2):
            shares = gathered.at[which, back(1 - which, d)]
            remote(shares, shares, sent5.at[which, d], got5.at[which, d], (sibling, sec)).wait_recv()
            pass_copy(core, which, d).start()
            keep_copy(which, d).start()
    for which in range(2):
        for d in range(4):
            pass_copy(1 - core, which, d).wait_recv()

    near_copy().wait_send()
    for c in range(CHUNKS):

        @pl.when(has_far)
        def _(c=c):
            far_copy(c).wait_send()

    for d in range(1, 16):
        cross_send(lax.rem(sec + d, 16)).wait_send()
    for i in range(W):
        owner, _, copy = axial_copy(i)

        @pl.when(owner != seg)
        def _(copy=copy):
            copy.wait_send()

    for d in range(1, 8):
        layer_copy(d).wait_send()
    for which in range(2):
        for d in range(1, 4):
            one_copy(which, d).wait_send()
            four_copy(which, d).wait_send()
        for d in range(4):
            pass_copy(core, which, d).wait_send()
            keep_copy(which, d).wait()


def fused(live, cols, coarse, prolong, operator):
    dma = pltpu.SemaphoreType.DMA
    vmem = pl.BlockSpec(memory_space=pltpu.VMEM)
    anywhere = pl.BlockSpec(memory_space=pl.ANY)
    bf16, f32, i32 = jnp.bfloat16, jnp.float32, jnp.int32
    return pl.pallas_call(
        fused_kernel,
        out_shape=jax.ShapeDtypeStruct((2, 2, 4, 4, 96, 128), bf16),
        in_specs=[pl.BlockSpec(memory_space=pltpu.SMEM), vmem, anywhere, anywhere, anywhere],
        out_specs=anywhere,
        scratch_shapes=[
            pltpu.VMEM((3, 4, 128), i32),
            pltpu.VMEM((5, 8, 128), i32),
            pltpu.VMEM((ROWS, 64, 256), bf16),
            pltpu.VMEM((ROWS, 64, 256), bf16),
            pltpu.VMEM((ROWS, 64, 256), bf16),
            pltpu.VMEM((2, 16, 8, 64, 64), bf16),
            pltpu.VMEM((ROWS, 64, 512), bf16),
            pltpu.VMEM((4 * ROWS + 1, 64, 128), bf16),
            pltpu.VMEM((3 * ROWS, 64, 512), bf16),
            pltpu.VMEM((512, 384), bf16),
            pltpu.VMEM((8, 384, 512), bf16),
            pltpu.VMEM((ROWS * 64, 512), f32),
            pltpu.VMEM((ROWS * 64, 512), bf16),
            pltpu.VMEM((384, 256), f32),
            pltpu.VMEM((2, 4, 4, 96, 128), bf16),
            pltpu.VMEM((16, 80, 128), bf16),
            pltpu.VMEM((16, 80, 128), bf16),
            pltpu.VMEM((16, 2, 16, 128), f32),
            pltpu.VMEM((256, 128), bf16),
            pltpu.VMEM((112, 128), f32),
            pltpu.SMEM((5, 8, 128), i32),
            dma((CHUNKS + 8,)),
            dma((CHUNKS + 1,)),
            dma((CHUNKS + 1,)),
            dma((16,)),
            dma((16,)),
            dma((W,)),
            dma((16, 2)),
            dma((8,)),
            dma((8,)),
            dma((2, 4)),
            dma((2, 4)),
            dma((2, 4)),
            dma((2, 4)),
            dma((2, 4)),
            dma((2, 4)),
            dma((2, 4)),
        ],
        compiler_params=pltpu.CompilerParams(collective_id=0, has_side_effects=True, vmem_limit_bytes=61 * 2**20),
        name="fused",
    )(live, cols, coarse, prolong, operator)


def place_kernel(first_share, second_share, out_ref):
    half, low_y = pl.program_id(0) // 2, lax.rem(pl.program_id(0), 2) * 2
    out_ref[...] = jnp.zeros_like(out_ref)
    for j in range(2):
        y = low_y + j
        first = jnp.where(half == 0, y // 3, jnp.minimum(3 + y, 4))
        for x in range(4):
            for unit in range(12):
                row = pl.multiple_of((first + unit) * 64 + x * 16, 16)
                rows = slice(unit % 6 * 16, unit % 6 * 16 + 16)
                value = first_share[0, 0, j, x, rows, :] if unit < 6 else second_share[0, 0, x, j, rows, :]
                out_ref[pl.ds(row, 16), 128 * j : 128 * j + 128] = value.astype(jnp.float32)


def place(shares):
    return pl.pallas_call(
        place_kernel,
        grid=(4,),
        out_shape=jax.ShapeDtypeStruct((1024, 1024), jnp.float32),
        in_specs=[
            pl.BlockSpec((1, 1, 2, 4, 96, 128), lambda i: (i // 2, 0, i % 2, 0, 0, 0)),
            pl.BlockSpec((1, 1, 4, 2, 96, 128), lambda i: (i // 2, 1, 0, i % 2, 0, 0)),
        ],
        out_specs=pl.BlockSpec((1024, 256), lambda i: (0, i)),
        compiler_params=pltpu.CompilerParams(vmem_limit_bytes=16 * 2**20),
        name="place",
    )(shares, shares)


def on_device(operator_blocks, prolong_blocks, operator_cols, coarse_map, live_rows):
    shares = fused(live_rows, operator_cols[0, 0].T, coarse_map.T, prolong_blocks[0, 0], operator_blocks[0, 0])
    return place(shares)


def solution(mesh):
    return jax.shard_map(
        on_device,
        mesh=mesh,
        in_specs=(
            P("axial", "cross", None, None, None, None),
            P("axial", "cross", None, None, None),
            P("axial", "cross", None, None),
            P(),
            P("axial", "cross"),
        ),
        out_specs=P(),
        check_vma=False,
    )
```

time: 84.4 us -> 82.2 us (0.974)
  Pallas kernels: 82.2 us -> 80 us
    pallas_call x1, Pallas kernels: 79.7 us -> 77.2 us  [fused(): pl.pallas_call(fused_kernel, out_shape=jax.ShapeDtypeStruct((2, 2, 4, 4,...]
where the time goes in v3:
time: 82.2 us; the launch traced here: 82.1 us
  Pallas kernels  80 us (97%)
  local copies, waits for them, and re-layouts  1.4 us (2%)
    pallas_call x1, Pallas kernels, fused(): pl.pallas_call(fused_kernel, out_shape=jax.ShapeDtypeStruct((2, 2, 4, 4,...  77.2 us
    pallas_call x1, Pallas kernels, place(): pl.pallas_call(place_kernel, grid=(4,), out_shape=jax.ShapeDtypeStruct((1...  2.77 us

profile of v3, /device:TPU:1, one launch (start us, length us, event | category | flops | bytes accessed | tf_op | source)
XLA Modules:
  0.0 82.1 jit_solution(13012205377543025041)
XLA Ops:
  0.7 77.2 %fused.1.first_share.second_share = bf16[2,2,4,4,96,128]{5,4,3,2,1,0:T(8,128)(2,1)} custom-call(s32[1,1]{1,0:T(1,128)S(6)} %copy.6.live, s32[8,64]{1,0:T(8,128)} %bitcast.9, s32[4,16384]{1,0:T(4,128)} %bitcast.8, bf16[64,64,256]{2,1,0:T(8,128)(2,1)} %bitcast.7, bf16[64,8,64,64]{3,2,1,0:T(8,128)(2,1)} %bitcast.6), custom_call_target="tpu_custom_call" | custom-call | tf_op jit(solution)/shard_map/fused/pallas_call | solution.py:375
  77.9 0.0 copy-start
  77.9 1.4 %copy-done = bf16[2,2,4,4,96,128]{5,4,3,2,1,0:T(8,128)(2,1)S(1)} copy-done((bf16[2,2,4,4,96,128]{5,4,3,2,1,0:T(8,128)(2,1)S(1)}, bf16[2,2,4,4,96,128]{5,4,3,2,1,0:T(8,128)(2,1)}, u32[]{:S(2)}) %copy-start) | copy-done | bytes 1572888
  79.3 2.8 %place.1 = f32[1024,1024]{1,0:T(8,128)} custom-call(bf16[2,2,4,4,96,128]{5,4,3,2,1,0:T(8,128)(2,1)S(1)} %copy-done, bf16[2,2,4,4,96,128]{5,4,3,2,1,0:T(8,128)(2,1)S(1)} %copy-done), custom_call_target="tpu_custom_call" | custom-call | tf_op jit(solution)/shard_map/place/pallas_call | solution.py:439
Async XLA Ops:
  77.9 1.4 %copy-start = (bf16[2,2,4,4,96,128]{5,4,3,2,1,0:T(8,128)(2,1)S(1)}, bf16[2,2,4,4,96,128]{5,4,3,2,1,0:T(8,128)(2,1)}, u32[]{:S(2)}) copy-start(bf16[2,2,4,4,96,128]{5,4,3,2,1,0:T(8,128)(2,1)} %fused.1.first_share.second_share) | copy-start | bytes 4718596

commit v4 on v3

--- a/solution.py
+++ b/solution.py
@@ -8,7 +8,7 @@
 NCB = 16
 W = 5
 ROWS = 64
-PIECES = ((0, 32), (32, 48), (48, 64))
+PIECES = ((0, 32), (32, 64))
 CHUNKS = len(PIECES)
 MESH = pl.DeviceIdType.MESH
 EMPTY = 4 * ROWS
@@ -185,7 +185,7 @@
             store_tiles(far, lo, hi)
             widen(2, lo, hi)
 
-        @pl.loop(0, ROWS, unroll=4)
+        @pl.loop(0, ROWS, unroll=8)
         def _(row, c=c, lo=lo, hi=hi):
             rhs = jnp.concatenate([wide[tab_s[4, k, row], lo:hi, :] for k in range(8)], axis=0)
             term = jnp.dot(beside[row, :, 8 * lo : 8 * hi], rhs, preferred_element_type=jnp.float32)
@@ -445,7 +445,7 @@
             pl.BlockSpec((1, 1, 4, 2, 96, 128), lambda i: (i // 2, 1, 0, i % 2, 0, 0)),
         ],
         out_specs=pl.BlockSpec((1024, 256), lambda i: (0, i)),
-        compiler_params=pltpu.CompilerParams(vmem_limit_bytes=16 * 2**20),
+        compiler_params=pltpu.CompilerParams(vmem_limit_bytes=61 * 2**20),
         name="place",
     )(shares, shares)
 

time: 82.2 us -> 78.2 us (0.951)
  Pallas kernels: 80 us -> 77.3 us
  local copies, waits for them, and re-layouts: 1.4 us -> 0 us
    pallas_call x1, Pallas kernels: 77.2 us -> 72.9 us  [fused(): pl.pallas_call(fused_kernel, out_shape=jax.ShapeDtypeStruct((2, 2, 4, 4,...]
    pallas_call x1, Pallas kernels: 2.77 us -> 4.38 us  [place(): pl.pallas_call(place_kernel, grid=(4,), out_shape=jax.ShapeDtypeStruct((1...]
    unnamed x2 -> x0, local copies, waits for them, and re-layouts: 1.4 us -> none
where the time goes in v4:
time: 78.2 us; the launch traced here: 78 us
  Pallas kernels  77.3 us (99%)
    pallas_call x1, Pallas kernels, fused(): pl.pallas_call(fused_kernel, out_shape=jax.ShapeDtypeStruct((2, 2, 4, 4,...  72.9 us
    pallas_call x1, Pallas kernels, place(): pl.pallas_call(place_kernel, grid=(4,), out_shape=jax.ShapeDtypeStruct((1...  4.38 us

profile of v4, /device:TPU:1, one launch (start us, length us, event | category | flops | bytes accessed | tf_op | source)
XLA Modules:
  0.0 78.0 jit_solution(13557897281906320771)
XLA Ops:
  0.7 72.9 %fused.1.first_share.second_share = bf16[2,2,4,4,96,128]{5,4,3,2,1,0:T(8,128)(2,1)} custom-call(s32[1,1]{1,0:T(1,128)S(6)} %copy.6.live, s32[8,64]{1,0:T(8,128)} %bitcast.9, s32[4,16384]{1,0:T(4,128)} %bitcast.8, bf16[64,64,256]{2,1,0:T(8,128)(2,1)} %bitcast.7, bf16[64,8,64,64]{3,2,1,0:T(8,128)(2,1)} %bitcast.6), custom_call_target="tpu_custom_call" | custom-call | tf_op jit(solution)/shard_map/fused/pallas_call | solution.py:375
  73.6 4.4 %place.1 = f32[1024,1024]{1,0:T(8,128)} custom-call(bf16[2,2,4,4,96,128]{5,4,3,2,1,0:T(8,128)(2,1)} %fused.1.first_share.second_share, bf16[2,2,4,4,96,128]{5,4,3,2,1,0:T(8,128)(2,1)} %fused.1.first_share.second_share), custom_call_target="tpu_custom_call" | custom-call | tf_op jit(solution)/shard_map/place/pallas_call | solution.py:439

commit v5 on v4

--- a/solution.py
+++ b/solution.py
@@ -130,7 +130,7 @@
         )
 
     def store_tiles(source, lo, hi):
-        @pl.loop(0, ROWS, unroll=4)
+        @pl.loop(0, ROWS, unroll=8)
         def _(row):
             value = source[row, lo:hi, :]
             for pair in range(2):
@@ -139,7 +139,7 @@
                 tiles[4 * row + 2 + pair, lo:hi, :] = jnp.concatenate([tile[:, 64:], tile[:, :64]], axis=1)
 
     def widen(part, lo, hi):
-        @pl.loop(0, ROWS, unroll=4)
+        @pl.loop(0, ROWS, unroll=8)
         def _(row):
             for pair in range(4):
                 wide[part * ROWS + row, lo:hi, 128 * pair : 128 * pair + 128] = half_tiles(part, row, pair, lo, hi)
@@ -185,7 +185,7 @@
             store_tiles(far, lo, hi)
             widen(2, lo, hi)
 
-        @pl.loop(0, ROWS, unroll=8)
+        @pl.loop(0, ROWS, unroll=16)
         def _(row, c=c, lo=lo, hi=hi):
             rhs = jnp.concatenate([wide[tab_s[4, k, row], lo:hi, :] for k in range(8)], axis=0)
             term = jnp.dot(beside[row, :, 8 * lo : 8 * hi], rhs, preferred_element_type=jnp.float32)
@@ -305,9 +305,9 @@
         share = gathered.at[which, major, minor]
         return remote(share, share, sent4.at[which, d], got4.at[which, d], moved(which, d))
 
-    def four_copy(which, d):
-        shares = gathered.at[which, y if which == 0 else x]
-        return remote(shares, shares, sent5.at[which, d], got5.at[which, d], moved(1 - which, d))
+    def next_copy(which, d, j):
+        share = gathered.at[which, y if which == 0 else x, back(which, j)]
+        return remote(share, share, sent5.at[which, d, j], got5.at[which, d, j], moved(1 - which, d))
 
     def pass_copy(half, which, d):
         place = back(1 - which, d)
@@ -321,19 +321,23 @@
     for d in (2, 1, 3):
         for which in range(2):
             one_copy(which, d).start()
-    for which in range(2):
-        for d in (1, 3, 2):
-            share = gathered.at[which, y if which == 0 else x, back(which, d)]
-            remote(share, share, sent4.at[which, d], got4.at[which, d], (sibling, sec)).wait_recv()
-        for d in (2, 1, 3):
-            four_copy(which, d).start()
+    for d in (2, 1, 3):
+        for which in range(2):
+            next_copy(which, d, 0).start()
+    for j in (1, 3, 2):
+        for which in range(2):
+            share = gathered.at[which, y if which == 0 else x, back(which, j)]
+            remote(share, share, sent4.at[which, j], got4.at[which, j], (sibling, sec)).wait_recv()
+            for d in (2, 1, 3):
+                next_copy(which, d, j).start()
     for which in range(2):
         pass_copy(core, which, 0).start()
         keep_copy(which, 0).start()
     for d in (1, 3, 2):
         for which in range(2):
-            shares = gathered.at[which, back(1 - which, d)]
-            remote(shares, shares, sent5.at[which, d], got5.at[which, d], (sibling, sec)).wait_recv()
+            for j in (0, 1, 3, 2):
+                share = gathered.at[which, back(1 - which, d), back(which, j)]
+                remote(share, share, sent5.at[which, d, j], got5.at[which, d, j], (sibling, sec)).wait_recv()
             pass_copy(core, which, d).start()
             keep_copy(which, d).start()
     for which in range(2):
@@ -361,7 +365,8 @@
     for which in range(2):
         for d in range(1, 4):
             one_copy(which, d).wait_send()
-            four_copy(which, d).wait_send()
+            for j in range(4):
+                next_copy(which, d, j).wait_send()
         for d in range(4):
             pass_copy(core, which, d).wait_send()
             keep_copy(which, d).wait()
@@ -410,8 +415,8 @@
             dma((8,)),
             dma((2, 4)),
             dma((2, 4)),
-            dma((2, 4)),
-            dma((2, 4)),
+            dma((2, 4, 4)),
+            dma((2, 4, 4)),
             dma((2, 4)),
             dma((2, 4)),
             dma((2, 4)),
@@ -421,33 +426,56 @@
     )(live, cols, coarse, prolong, operator)
 
 
-def place_kernel(first_share, second_share, out_ref):
-    half, low_y = pl.program_id(0) // 2, lax.rem(pl.program_id(0), 2) * 2
-    out_ref[...] = jnp.zeros_like(out_ref)
-    for j in range(2):
-        y = low_y + j
-        first = jnp.where(half == 0, y // 3, jnp.minimum(3 + y, 4))
-        for x in range(4):
-            for unit in range(12):
-                row = pl.multiple_of((first + unit) * 64 + x * 16, 16)
-                rows = slice(unit % 6 * 16, unit % 6 * 16 + 16)
-                value = first_share[0, 0, j, x, rows, :] if unit < 6 else second_share[0, 0, x, j, rows, :]
-                out_ref[pl.ds(row, 16), 128 * j : 128 * j + 128] = value.astype(jnp.float32)
+def place_kernel(shares, out_ref, held, dense, got, gone):
+    loads = [pltpu.make_async_copy(shares.at[i // 2, i % 2], held.at[i // 2, i % 2], got.at[i]) for i in range(4)]
+    for load in loads:
+        load.start()
+    windows = {(half, y): y // 3 if half == 0 else min(3 + y, 4) for half in range(2) for y in range(4)}
+    for (half, y), first in windows.items():
+        column = (y + 4 * half) * 128
+        for start, end in ((0, first * 64), ((first + 12) * 64, 1024)):
+            if end > start:
+                dense[start:end, column : column + 128] = jnp.zeros((end - start, 128), jnp.float32)
+    for load in loads:
+        load.wait()
+
+    def store(part):
+        rows = pl.ds(part * 128, 128)
+        return pltpu.make_async_copy(dense.at[rows], out_ref.at[rows], gone.at[part])
+
+    for part in range(8):
+        for block in (2 * part, 2 * part + 1):
+            for (half, y), first in windows.items():
+                unit, column = block - first, (y + 4 * half) * 128
+                if not 0 <= unit < 12:
+                    continue
+                for x in range(4):
+                    row = block * 64 + x * 16
+                    at = (half, 0, y, x) if unit < 6 else (half, 1, x, y)
+                    dense[row : row + 16, column : column + 128] = held[
+                        (*at, slice(unit % 6 * 16, unit % 6 * 16 + 16), slice(None))
+                    ].astype(jnp.float32)
+        store(part).start()
+    for part in range(8):
+        store(part).wait()
 
 
 def place(shares):
+    anywhere = pl.BlockSpec(memory_space=pl.ANY)
     return pl.pallas_call(
         place_kernel,
-        grid=(4,),
         out_shape=jax.ShapeDtypeStruct((1024, 1024), jnp.float32),
-        in_specs=[
-            pl.BlockSpec((1, 1, 2, 4, 96, 128), lambda i: (i // 2, 0, i % 2, 0, 0, 0)),
-            pl.BlockSpec((1, 1, 4, 2, 96, 128), lambda i: (i // 2, 1, 0, i % 2, 0, 0)),
+        in_specs=[anywhere],
+        out_specs=anywhere,
+        scratch_shapes=[
+            pltpu.VMEM((2, 2, 4, 4, 96, 128), jnp.bfloat16),
+            pltpu.VMEM((1024, 1024), jnp.float32),
+            pltpu.SemaphoreType.DMA((4,)),
+            pltpu.SemaphoreType.DMA((8,)),
         ],
-        out_specs=pl.BlockSpec((1024, 256), lambda i: (0, i)),
         compiler_params=pltpu.CompilerParams(vmem_limit_bytes=61 * 2**20),
         name="place",
-    )(shares, shares)
+    )(shares)
 
 
 def on_device(operator_blocks, prolong_blocks, operator_cols, coarse_map, live_rows):

time: 78.2 us -> 75.6 us (0.967)
  Pallas kernels: 77.3 us -> 74.8 us
    pallas_call x1, Pallas kernels: 72.9 us -> 71.3 us  [fused(): pl.pallas_call(fused_kernel, out_shape=jax.ShapeDtypeStruct((2, 2, 4, 4,...]
    pallas_call x1, Pallas kernels: 4.38 us -> 3.47 us  [place(): pl.pallas_call(place_kernel, out_shape=jax.ShapeDtypeStruct((1024, 1024),...]
where the time goes in v5:
time: 75.6 us; the launch traced here: 75.4 us
  Pallas kernels  74.8 us (99%)
    pallas_call x1, Pallas kernels, fused(): pl.pallas_call(fused_kernel, out_shape=jax.ShapeDtypeStruct((2, 2, 4, 4,...  71.3 us
    pallas_call x1, Pallas kernels, place(): pl.pallas_call(place_kernel, out_shape=jax.ShapeDtypeStruct((1024, 1024),...  3.47 us

profile of v5, /device:TPU:1, one launch (start us, length us, event | category | flops | bytes accessed | tf_op | source)
XLA Modules:
  0.0 75.4 jit_solution(9755738415599015448)
XLA Ops:
  0.7 71.3 %fused.1.shares = bf16[2,2,4,4,96,128]{5,4,3,2,1,0:T(8,128)(2,1)} custom-call(s32[1,1]{1,0:T(1,128)S(6)} %copy.6.live, s32[8,64]{1,0:T(8,128)} %bitcast.9, s32[4,16384]{1,0:T(4,128)} %bitcast.8, bf16[64,64,256]{2,1,0:T(8,128)(2,1)} %bitcast.7, bf16[64,8,64,64]{3,2,1,0:T(8,128)(2,1)} %bitcast.6), custom_call_target="tpu_custom_call" | custom-call | tf_op jit(solution)/shard_map/fused/pallas_call | solution.py:380
  72.0 3.5 %place.1 = f32[1024,1024]{1,0:T(8,128)} custom-call(bf16[2,2,4,4,96,128]{5,4,3,2,1,0:T(8,128)(2,1)} %fused.1.shares), custom_call_target="tpu_custom_call" | custom-call | tf_op jit(solution)/shard_map/place/pallas_call | solution.py:465

commit v6 on v5

--- a/solution.py
+++ b/solution.py
@@ -8,7 +8,7 @@
 NCB = 16
 W = 5
 ROWS = 64
-PIECES = ((0, 32), (32, 64))
+PIECES = ((0, 32), (32, 48), (48, 64))
 CHUNKS = len(PIECES)
 MESH = pl.DeviceIdType.MESH
 EMPTY = 4 * ROWS
@@ -25,7 +25,7 @@
 
 def fused_kernel(
     live, cols_ref, map_ref, p_ref, a_ref, shares_out,
-    maps, tab, own, near, far, blocks, beside, tiles, wide, left, turned, partial, product, total, gathered,
+    maps, tab, own, near, far, blocks, beside, tiles, wide, left, turned, partial, partial2, product, total, gathered,
     chunks, from_cross, from_axial, ready, units,
     tab_s, load, sent0, got0, sent1, got1, sent2, got2, sent3, got3, sent4, got4, sent5, got5, sent6, got6, flush,
 ):
@@ -177,6 +177,8 @@
     store_tiles(near, 0, 64)
     widen(1, 0, 64)
 
+    sums = (partial, partial2)
+
     for c, (lo, hi) in enumerate(PIECES):
 
         @pl.when(has_far)
@@ -191,9 +193,9 @@
             term = jnp.dot(beside[row, :, 8 * lo : 8 * hi], rhs, preferred_element_type=jnp.float32)
             at = pl.ds(pl.multiple_of(row * 64, 64), 64)
             if c > 0:
-                term = partial[at, :] + term
+                term = sums[c - 1][at, :] + term
             if c < CHUNKS - 1:
-                partial[at, :] = term
+                sums[c][at, :] = term
             else:
                 product[at, :] = term.astype(jnp.bfloat16)
 
@@ -258,7 +260,10 @@
         def _(i=i, place=place):
             from_axial[seg, place] = units[16 * i : 16 * i + 16, :]
 
-    @pl.loop(0, 16)
+    first_source = jnp.where(2 * layer <= 4, 0, 2 * layer - 3)
+    end_source = jnp.where(2 * layer + 1 >= NCB - W, 16, 2 * layer + 3)
+
+    @pl.loop(first_source, end_source)
     def _(source):
         low = lowest_of(source)
         for place in range(2):
@@ -394,6 +399,7 @@
             pltpu.VMEM((3 * ROWS, 64, 512), bf16),
             pltpu.VMEM((512, 384), bf16),
             pltpu.VMEM((8, 384, 512), bf16),
+            pltpu.VMEM((ROWS * 64, 512), f32),
             pltpu.VMEM((ROWS * 64, 512), f32),
             pltpu.VMEM((ROWS * 64, 512), bf16),
             pltpu.VMEM((384, 256), f32),
@@ -436,28 +442,30 @@
         for start, end in ((0, first * 64), ((first + 12) * 64, 1024)):
             if end > start:
                 dense[start:end, column : column + 128] = jnp.zeros((end - start, 128), jnp.float32)
-    for load in loads:
-        load.wait()
-
-    def store(part):
-        rows = pl.ds(part * 128, 128)
-        return pltpu.make_async_copy(dense.at[rows], out_ref.at[rows], gone.at[part])
-
-    for part in range(8):
-        for block in (2 * part, 2 * part + 1):
-            for (half, y), first in windows.items():
-                unit, column = block - first, (y + 4 * half) * 128
-                if not 0 <= unit < 12:
-                    continue
-                for x in range(4):
-                    row = block * 64 + x * 16
-                    at = (half, 0, y, x) if unit < 6 else (half, 1, x, y)
-                    dense[row : row + 16, column : column + 128] = held[
-                        (*at, slice(unit % 6 * 16, unit % 6 * 16 + 16), slice(None))
-                    ].astype(jnp.float32)
-        store(part).start()
-    for part in range(8):
-        store(part).wait()
+
+    def store(half, part):
+        area = (pl.ds(part * 256, 256), pl.ds(half * 512, 512))
+        return pltpu.make_async_copy(dense.at[area], out_ref.at[area], gone.at[half, part])
+
+    for half in range(2):
+        loads[2 * half].wait()
+        loads[2 * half + 1].wait()
+        for part in range(4):
+            for block in range(4 * part, 4 * part + 4):
+                for y in range(4):
+                    unit, column = block - windows[half, y], (y + 4 * half) * 128
+                    if not 0 <= unit < 12:
+                        continue
+                    for x in range(4):
+                        row = block * 64 + x * 16
+                        at = (half, 0, y, x) if unit < 6 else (half, 1, x, y)
+                        dense[row : row + 16, column : column + 128] = held[
+                            (*at, slice(unit % 6 * 16, unit % 6 * 16 + 16), slice(None))
+                        ].astype(jnp.float32)
+            store(half, part).start()
+    for half in range(2):
+        for part in range(4):
+            store(half, part).wait()
 
 
 def place(shares):
@@ -471,7 +479,7 @@
             pltpu.VMEM((2, 2, 4, 4, 96, 128), jnp.bfloat16),
             pltpu.VMEM((1024, 1024), jnp.float32),
             pltpu.SemaphoreType.DMA((4,)),
-            pltpu.SemaphoreType.DMA((8,)),
+            pltpu.SemaphoreType.DMA((2, 4)),
         ],
         compiler_params=pltpu.CompilerParams(vmem_limit_bytes=61 * 2**20),
         name="place",

time: 75.6 us -> 73.6 us (0.974)
  Pallas kernels: 74.8 us -> 72.8 us
    pallas_call x1, Pallas kernels: 71.3 us -> 69.5 us  [fused(): pl.pallas_call(fused_kernel, out_shape=jax.ShapeDtypeStruct((2, 2, 4, 4,...]
where the time goes in v6:
time: 73.6 us; the launch traced here: 73.4 us
  Pallas kernels  72.8 us (99%)
    pallas_call x1, Pallas kernels, fused(): pl.pallas_call(fused_kernel, out_shape=jax.ShapeDtypeStruct((2, 2, 4, 4,...  69.5 us
    pallas_call x1, Pallas kernels, place(): pl.pallas_call(place_kernel, out_shape=jax.ShapeDtypeStruct((1024, 1024),...  3.25 us

profile of v6, /device:TPU:1, one launch (start us, length us, event | category | flops | bytes accessed | tf_op | source)
XLA Modules:
  0.0 73.4 jit_solution(4246802329271242155)
XLA Ops:
  0.7 69.5 %fused.1.shares = bf16[2,2,4,4,96,128]{5,4,3,2,1,0:T(8,128)(2,1)} custom-call(s32[1,1]{1,0:T(1,128)S(6)} %copy.6.live, s32[8,64]{1,0:T(8,128)} %bitcast.9, s32[4,16384]{1,0:T(4,128)} %bitcast.8, bf16[64,64,256]{2,1,0:T(8,128)(2,1)} %bitcast.7, bf16[64,8,64,64]{3,2,1,0:T(8,128)(2,1)} %bitcast.6), custom_call_target="tpu_custom_call" | custom-call | tf_op jit(solution)/shard_map/fused/pallas_call | solution.py:385
  70.2 3.3 %place.1 = f32[1024,1024]{1,0:T(8,128)} custom-call(bf16[2,2,4,4,96,128]{5,4,3,2,1,0:T(8,128)(2,1)} %fused.1.shares), custom_call_target="tpu_custom_call" | custom-call | tf_op jit(solution)/shard_map/place/pallas_call | solution.py:473

commit v7 on v6

--- a/solution.py
+++ b/solution.py
@@ -10,6 +10,7 @@
 ROWS = 64
 PIECES = ((0, 32), (32, 48), (48, 64))
 CHUNKS = len(PIECES)
+UNROLL = 32
 MESH = pl.DeviceIdType.MESH
 EMPTY = 4 * ROWS
 
@@ -155,7 +156,7 @@
                 left[64 * inner : 64 * inner + 64, 128 * pair : 128 * pair + 128] = half_tiles(
                     3, group * 8 + inner, pair, 0, 64
                 )
-        turned[group] = left[...].T
+        turned[group] = left[...].T[:320]
 
     for c in range(4):
         block_load(c).wait()
@@ -187,7 +188,7 @@
             store_tiles(far, lo, hi)
             widen(2, lo, hi)
 
-        @pl.loop(0, ROWS, unroll=16)
+        @pl.loop(0, ROWS, unroll=UNROLL)
         def _(row, c=c, lo=lo, hi=hi):
             rhs = jnp.concatenate([wide[tab_s[4, k, row], lo:hi, :] for k in range(8)], axis=0)
             term = jnp.dot(beside[row, :, 8 * lo : 8 * hi], rhs, preferred_element_type=jnp.float32)
@@ -398,11 +399,11 @@
             pltpu.VMEM((4 * ROWS + 1, 64, 128), bf16),
             pltpu.VMEM((3 * ROWS, 64, 512), bf16),
             pltpu.VMEM((512, 384), bf16),
-            pltpu.VMEM((8, 384, 512), bf16),
+            pltpu.VMEM((8, 320, 512), bf16),
             pltpu.VMEM((ROWS * 64, 512), f32),
             pltpu.VMEM((ROWS * 64, 512), f32),
             pltpu.VMEM((ROWS * 64, 512), bf16),
-            pltpu.VMEM((384, 256), f32),
+            pltpu.VMEM((320, 256), f32),
             pltpu.VMEM((2, 4, 4, 96, 128), bf16),
             pltpu.VMEM((16, 80, 128), bf16),
             pltpu.VMEM((16, 80, 128), bf16),

time: 73.6 us -> 72.4 us (0.984)
  Pallas kernels: 72.8 us -> 71.6 us
    pallas_call x1, Pallas kernels: 69.5 us -> 68.3 us  [fused(): pl.pallas_call(fused_kernel, out_shape=jax.ShapeDtypeStruct((2, 2, 4, 4,...]
where the time goes in v7:
time: 72.4 us; the launch traced here: 72.2 us
  Pallas kernels  71.6 us (99%)
    pallas_call x1, Pallas kernels, fused(): pl.pallas_call(fused_kernel, out_shape=jax.ShapeDtypeStruct((2, 2, 4, 4,...  68.3 us
    pallas_call x1, Pallas kernels, place(): pl.pallas_call(place_kernel, out_shape=jax.ShapeDtypeStruct((1024, 1024),...  3.25 us

profile of v7, /device:TPU:1, one launch (start us, length us, event | category | flops | bytes accessed | tf_op | source)
XLA Modules:
  0.0 72.2 jit_solution(17250330182690138255)
XLA Ops:
  0.7 68.3 %fused.1.shares = bf16[2,2,4,4,96,128]{5,4,3,2,1,0:T(8,128)(2,1)} custom-call(s32[1,1]{1,0:T(1,128)S(6)} %copy.6.live, s32[8,64]{1,0:T(8,128)} %bitcast.9, s32[4,16384]{1,0:T(4,128)} %bitcast.8, bf16[64,64,256]{2,1,0:T(8,128)(2,1)} %bitcast.7, bf16[64,8,64,64]{3,2,1,0:T(8,128)(2,1)} %bitcast.6), custom_call_target="tpu_custom_call" | custom-call | tf_op jit(solution)/shard_map/fused/pallas_call | solution.py:386
  69.0 3.3 %place.1 = f32[1024,1024]{1,0:T(8,128)} custom-call(bf16[2,2,4,4,96,128]{5,4,3,2,1,0:T(8,128)(2,1)} %fused.1.shares), custom_call_target="tpu_custom_call" | custom-call | tf_op jit(solution)/shard_map/place/pallas_call | solution.py:474

commit v8 on v7

--- a/solution.py
+++ b/solution.py
@@ -10,6 +10,7 @@
 ROWS = 64
 PIECES = ((0, 32), (32, 48), (48, 64))
 CHUNKS = len(PIECES)
+PARTS = 4
 UNROLL = 32
 MESH = pl.DeviceIdType.MESH
 EMPTY = 4 * ROWS
@@ -47,42 +48,46 @@
             src_ref=src, dst_ref=dst, send_sem=send, recv_sem=recv, device_id=to, device_id_type=MESH
         )
 
+    def part_of(ref, c):
+        return ref.at[:, pl.ds(16 * c, 16), :]
+
+    own_loads = [pltpu.make_async_copy(part_of(p_ref, c), part_of(own, c), load.at[c]) for c in range(PARTS)]
+    own_loads[0].start()
     barrier = pltpu.get_barrier_semaphore()
+    pl.semaphore_signal(barrier, inc=1, device_id=(lax.rem(seg + 1, 16), sec), device_id_type=MESH)
+    pl.semaphore_signal(barrier, inc=1, device_id=(lax.rem(seg + 15, 16), sec), device_id_type=MESH)
+    for copy in own_loads[1:]:
+        copy.start()
     for d in range(1, 16):
-        pl.semaphore_signal(barrier, inc=1, device_id=(lax.rem(seg + d, 16), sec), device_id_type=MESH)
+        if 1 < d < 15:
+            pl.semaphore_signal(barrier, inc=1, device_id=(lax.rem(seg + d, 16), sec), device_id_type=MESH)
         pl.semaphore_signal(barrier, inc=1, device_id=(seg, lax.rem(sec + d, 16)), device_id_type=MESH)
 
-    def piece(ref, c):
-        return ref.at[:, pl.ds(PIECES[c][0], PIECES[c][1] - PIECES[c][0]), :]
-
-    own_loads = [pltpu.make_async_copy(piece(p_ref, c), piece(own, c), load.at[c]) for c in range(CHUNKS)]
-    for copy in own_loads:
-        copy.start()
     map_loads = []
     for part, near_seg in enumerate((seg, sibling, beyond)):
         start = pl.multiple_of((near_seg * 16 + sec - lax.rem(sec, 2)) * ROWS, 128)
-        map_loads.append(pltpu.make_async_copy(map_ref.at[:, pl.ds(start, 128)], maps.at[part], load.at[CHUNKS + part]))
+        map_loads.append(pltpu.make_async_copy(map_ref.at[:, pl.ds(start, 128)], maps.at[part], load.at[PARTS + part]))
         map_loads[part].start()
 
     def block_load(c):
-        return pltpu.make_async_copy(a_ref.at[pl.ds(16 * c, 16)], blocks.at[c % 2], load.at[CHUNKS + 3 + c])
+        return pltpu.make_async_copy(a_ref.at[pl.ds(16 * c, 16)], blocks.at[c % 2], load.at[PARTS + 3 + c])
 
     for c in range(2):
         block_load(c).start()
 
     def near_copy():
-        return remote(own, near, sent0.at[CHUNKS], got0.at[CHUNKS], (sibling, sec))
+        return remote(own, near, sent0.at[PARTS], got0.at[PARTS], (sibling, sec))
 
     def far_copy(c):
-        return remote(piece(own, c), piece(far, c), sent0.at[c], got0.at[c], (beyond, sec))
+        return remote(part_of(own, c), part_of(far, c), sent0.at[c], got0.at[c], (beyond, sec))
 
     in_use = live[0, 0]
-    for c, (lo, hi) in enumerate(PIECES):
+    for c in range(PARTS):
         own_loads[c].wait()
 
         @pl.loop(0, ROWS, unroll=8)
-        def _(row, lo=lo, hi=hi):
-            own[row, lo:hi, :] = jnp.where(row < in_use, own[row, lo:hi, :], jnp.zeros((hi - lo, 256), jnp.bfloat16))
+        def _(row, rows=slice(16 * c, 16 * c + 16)):
+            own[row, rows, :] = jnp.where(row < in_use, own[row, rows, :], jnp.zeros((16, 256), jnp.bfloat16))
 
         if c == 0:
             pl.semaphore_wait(barrier, 30)
@@ -117,7 +122,7 @@
     part = jnp.where(named_seg == seg, 0, jnp.where(named_seg == sibling, 1, 2))
     tab[4, :, 0:64] = part * ROWS + (named & 63)
     tab[4, :, 64:128] = jnp.zeros((8, 64), jnp.int32)
-    to_smem = pltpu.make_async_copy(tab, tab_s, load.at[CHUNKS + 7])
+    to_smem = pltpu.make_async_copy(tab, tab_s, load.at[PARTS + 7])
     to_smem.start()
 
     lane_low = lax.broadcasted_iota(jnp.int32, (64, 128), 1) < 64
@@ -184,7 +189,8 @@
 
         @pl.when(has_far)
         def _(c=c, lo=lo, hi=hi):
-            far_copy(c).wait_recv()
+            for part in range(lo // 16, hi // 16):
+                far_copy(part).wait_recv()
             store_tiles(far, lo, hi)
             widen(2, lo, hi)
 
@@ -351,7 +357,7 @@
             pass_copy(1 - core, which, d).wait_recv()
 
     near_copy().wait_send()
-    for c in range(CHUNKS):
+    for c in range(PARTS):
 
         @pl.when(has_far)
         def _(c=c):
@@ -411,9 +417,9 @@
             pltpu.VMEM((256, 128), bf16),
             pltpu.VMEM((112, 128), f32),
             pltpu.SMEM((5, 8, 128), i32),
-            dma((CHUNKS + 8,)),
-            dma((CHUNKS + 1,)),
-            dma((CHUNKS + 1,)),
+            dma((PARTS + 8,)),
+            dma((PARTS + 1,)),
+            dma((PARTS + 1,)),
             dma((16,)),
             dma((16,)),
             dma((W,)),

time: 72.4 us -> 72.4 us (level)
  no operation moved by 1% of the time
where the time goes in v8:
time: 72.4 us; the launch traced here: 72.3 us
  Pallas kernels  71.6 us (99%)
    pallas_call x1, Pallas kernels, fused(): pl.pallas_call(fused_kernel, out_shape=jax.ShapeDtypeStruct((2, 2, 4, 4,...  68.4 us
    pallas_call x1, Pallas kernels, place(): pl.pallas_call(place_kernel, out_shape=jax.ShapeDtypeStruct((1024, 1024),...  3.25 us

profile of v8, /device:TPU:1, one launch (start us, length us, event | category | flops | bytes accessed | tf_op | source)
XLA Modules:
  0.0 72.3 jit_solution(1314830952856918785)
XLA Ops:
  0.7 68.4 %fused.1.shares = bf16[2,2,4,4,96,128]{5,4,3,2,1,0:T(8,128)(2,1)} custom-call(s32[1,1]{1,0:T(1,128)S(6)} %copy.6.live, s32[8,64]{1,0:T(8,128)} %bitcast.9, s32[4,16384]{1,0:T(4,128)} %bitcast.8, bf16[64,64,256]{2,1,0:T(8,128)(2,1)} %bitcast.7, bf16[64,8,64,64]{3,2,1,0:T(8,128)(2,1)} %bitcast.6), custom_call_target="tpu_custom_call" | custom-call | tf_op jit(solution)/shard_map/fused/pallas_call | solution.py:392
  69.0 3.3 %place.1 = f32[1024,1024]{1,0:T(8,128)} custom-call(bf16[2,2,4,4,96,128]{5,4,3,2,1,0:T(8,128)(2,1)} %fused.1.shares), custom_call_target="tpu_custom_call" | custom-call | tf_op jit(solution)/shard_map/place/pallas_call | solution.py:480
